TPU v7x, 256 devices: a whole 4x4x8 slice. The times are simulated.
256 devices in a mesh: gx: 8 (over y, core), gy: 32 (over x, z).
Axes of the slice: x: 4, y: 4, z: 8, core: 2. Of those that a mesh axis runs over, the one named last changes fastest.
Arguments:
- right_side: float32 [64, 512, 512], P('gx', 'gy'), may hold values from -8 to 8
- inverse_density: float32 [64, 512, 512], P('gx', 'gy'), may hold values from 0.25 to 4
Outputs:
- correction: float32 [64, 512, 512], P('gx', 'gy')
All inputs are finite; a program needn't handle non-finite values.
Results may differ from a plain program's by a relative error of at most 0.0003.
Values sent between devices are 32-bit elements; how exact they have to be, the bound alone decides.
A program may use at most 64 MiB of HBM per device.

v0:
```python
import jax
import jax.numpy as jnp
from jax import lax
from jax.sharding import PartitionSpec as P

LEVELS = 4
DEGREE = 2


theta_mid = 1.25
delta_half = 0.75


def with_halo(block, sides, width):
    for axis, dim in sides:
        count = lax.axis_size(axis)
        forward = [(i, i + 1) for i in range(count - 1)]
        backward = [(target, source) for source, target in forward]
        low = lax.ppermute(
            lax.slice_in_dim(block, block.shape[dim] - width, None, axis=dim), axis, forward
        )
        high = lax.ppermute(lax.slice_in_dim(block, 0, width, axis=dim), axis, backward)
        block = jnp.concatenate([low, block, high], axis=dim)
    return block


def harmonic(first, second):
    return 2.0 * first * second / (first + second)


def face_weights(padded):
    inner = padded[1:-1, 1:-1]
    weight_x = harmonic(padded[:-1, 1:-1], padded[1:, 1:-1])
    weight_y = harmonic(padded[1:-1, :-1], padded[1:-1, 1:])
    weight_z = harmonic(inner[..., :-1], inner[..., 1:])
    return (weight_x, weight_y, weight_z)


def diag_of(weights, scale):
    weight_x, weight_y, weight_z = weights
    along_z = jnp.pad(weight_z, ((0, 0), (0, 0), (0, 1))) + jnp.pad(
        weight_z, ((0, 0), (0, 0), (1, 0))
    )
    return (weight_x[1:] + weight_x[:-1] + weight_y[:, 1:] + weight_y[:, :-1] + along_z) * scale


def stencil(padded, weights, scale):
    weight_x, weight_y, weight_z = weights
    inner = padded[1:-1, 1:-1]
    flux_x = weight_x * (padded[1:, 1:-1] - padded[:-1, 1:-1])
    flux_y = weight_y * (padded[1:-1, 1:] - padded[1:-1, :-1])
    flux_z = weight_z * (inner[..., 1:] - inner[..., :-1])
    spread = flux_x[1:] - flux_x[:-1] + flux_y[:, 1:] - flux_y[:, :-1]
    spread = (
        spread
        + jnp.pad(flux_z, ((0, 0), (0, 0), (0, 1)))
        - jnp.pad(flux_z, ((0, 0), (0, 0), (1, 0)))
    )
    return -scale * spread


def smooth(field, resid, operate, inv_diag, steps, need_resid):
    sigma = theta_mid / delta_half
    rho_now = 1.0 / sigma
    direction = inv_diag * resid / theta_mid
    for step in range(steps):
        field = field + direction
        if step + 1 < steps or need_resid:
            resid = resid - operate(direction)
        if step + 1 < steps:
            rho_next = 1.0 / (2.0 * sigma - rho_now)
            direction = (
                rho_next * rho_now * direction + 2.0 * rho_next / delta_half * inv_diag * resid
            )
            rho_now = rho_next
    return (field, resid)


def restrict(values):
    nx, ny, nz = values.shape
    return values.reshape(nx // 2, 2, ny // 2, 2, nz // 2, 2).mean(axis=(1, 3, 5))


def prolong(values):
    nx, ny, nz = values.shape
    grown = jnp.broadcast_to(values[:, None, :, None, :, None], (nx, 2, ny, 2, nz, 2))
    return grown.reshape(2 * nx, 2 * ny, 2 * nz)


def dct_matrix(count):
    wave = jnp.arange(count).astype(jnp.float32)[:, None]
    place = jnp.arange(count).astype(jnp.float32)[None, :]
    norms = jnp.where(wave == 0.0, jnp.sqrt(1.0 / count), jnp.sqrt(2.0 / count))
    return norms * jnp.cos(jnp.pi * wave * (2.0 * place + 1.0) / (2.0 * count))


def inverse_table(totals, starts, counts, scale):
    lam = []
    zeros = []
    for total, start, count in zip(totals, starts, counts):
        wave = (start + jnp.arange(count)).astype(jnp.float32)
        lam.append(2.0 - 2.0 * jnp.cos(jnp.pi * wave / total))
        zeros.append(wave == 0.0)
    lam_all = (lam[0][:, None, None] + lam[1][None, :, None] + lam[2][None, None, :]) * scale
    zero_all = zeros[0][:, None, None] & zeros[1][None, :, None] & zeros[2][None, None, :]
    return jnp.where(zero_all, 0.0, 1.0 / (lam_all + zero_all.astype(jnp.float32)))


def turn(matrix, values, form):
    return jnp.einsum(form, matrix, values, precision=lax.Precision.HIGHEST)


def coarse_solve(resid, scale):
    size_x = lax.axis_size("gx")
    size_y = lax.axis_size("gy")
    block_x, block_y, total_z = resid.shape
    total_x = block_x * size_x
    total_y = block_y * size_y
    mat_x, mat_y, mat_z = (dct_matrix(total_x), dct_matrix(total_y), dct_matrix(total_z))
    zero_start = jnp.zeros((), jnp.int32)
    part_z = total_z // size_y
    part_y = total_y // size_x
    coeffs = turn(mat_z, resid, "ck,abk->abc")
    coeffs = lax.all_to_all(coeffs, "gy", split_axis=2, concat_axis=1, tiled=True)
    coeffs = turn(mat_y, coeffs, "bj,ajc->abc")
    coeffs = lax.all_to_all(coeffs, "gx", split_axis=1, concat_axis=0, tiled=True)
    coeffs = turn(mat_x, coeffs, "ai,ibc->abc")
    table = inverse_table(
        (total_x, total_y, total_z),
        (zero_start, lax.axis_index("gx") * part_y, lax.axis_index("gy") * part_z),
        (total_x, part_y, part_z),
        scale,
    )
    coeffs = turn(mat_x, coeffs * table, "ai,abc->ibc")
    coeffs = lax.all_to_all(coeffs, "gx", split_axis=0, concat_axis=1, tiled=True)
    coeffs = turn(mat_y, coeffs, "bj,ibc->ijc")
    coeffs = lax.all_to_all(coeffs, "gy", split_axis=1, concat_axis=2, tiled=True)
    return turn(mat_z, coeffs, "ck,ijc->ijk")


def field_rim(values):
    return with_halo(values, (("gx", 0), ("gy", 1)), 1)


def density_rim(values):
    return with_halo(values, (("gx", 0), ("gy", 1)), 1)


def level_work(rhs, coef, scale, coef_rim, values_rim, lower):
    weights = face_weights(coef_rim(coef))
    inv_diag = 1.0 / diag_of(weights, scale)

    def operate(values):
        return stencil(values_rim(values), weights, scale)

    field, resid = smooth(jnp.zeros_like(rhs), rhs, operate, inv_diag, DEGREE, True)
    field = field + lower(resid)
    resid = rhs - operate(field)
    field, unused = smooth(field, resid, operate, inv_diag, DEGREE, False)
    return field


def cycle(rhs, coef, level):
    scale = 4.0 ** (-level)
    if level + 1 == LEVELS:
        return level_work(
            rhs, coef, scale, density_rim, field_rim, lambda resid: coarse_solve(resid, scale)
        )
    return level_work(
        rhs,
        coef,
        scale,
        density_rim,
        field_rim,
        lambda resid: prolong(cycle(restrict(resid), restrict(coef), level + 1)),
    )


def local(right_side, inverse_density):
    return cycle(right_side, inverse_density, 0)


def solution(mesh):
    return jax.shard_map(
        local,
        mesh=mesh,
        in_specs=(P("gx", "gy", None), P("gx", "gy", None)),
        out_specs=P("gx", "gy", None),
        check_vma=False,
    )
```

profile of v0, /device:TPU:10, one launch (start us, length us, event | category | flops | bytes accessed | tf_op | source)
XLA Modules:
  0.0 487.3 jit_solution(7225456549701002391)
XLA Ops:
  0.0 18.9 %reshape.217 = f32[4,2,8,2,256,2]{5,4,3,2,1,0:T(8,128)} reshape(f32[8,16,512]{2,1,0:T(8,128)} %param.3) | data formatting | bytes 524288 | tf_op jit(solution)/shard_map/reshape | solution.py:81
  18.9 7.0 %reduce_sum.68 = f32[4,8,256]{2,1,0:T(8,128)S(1)} reduce(f32[4,2,8,2,256,2]{5,4,3,2,1,0:T(8,128)} %reshape.217, f32[]{:T(128)} %constant.36.clone.1), dimensions={1,3,5}, to_apply=%region_0.1 | reduce | flops 57344 | bytes 294916 | tf_op jit(solution)/shard_map/reduce_sum | solution.py:81
  51.4 5.8 %collective-permute-start.35 = (f32[3,1,64]{2,1,0:T(1,128)S(1)}, f32[3,1,64]{2,1,0:T(1,128)S(1)}, u32[]{:S(2)}, u32[]{:S(2)}) collective-permute-start(f32[3,1,64]{2,1,0:T(1,128)S(1)} %get-tuple-element.107), channel_id=1, source_target_pairs={{1,0},{2,1},{3,2},{4,3},{5,4},{6,5},{7,6},{8,7},{9,8},{10,9},{11,1... | collective-permute-start | bytes 2312 | tf_op jit(solution)/shard_map/ppermute | solution.py:22
  66.6 6.0 %collective-permute-start.23 = (f32[4,1,128]{2,1,0:T(1,128)S(1)}, f32[4,1,128]{2,1,0:T(1,128)S(1)}, u32[]{:S(2)}, u32[]{:S(2)}) collective-permute-start(f32[4,1,128]{2,1,0:T(1,128)S(1)} %get-tuple-element.85), channel_id=1, source_target_pairs={{1,0},{2,1},{3,2},{4,3},{5,4},{6,5},{7,6},{8,7},{9,8},{10,9},{11,1... | collective-permute-start | bytes 6152 | tf_op jit(solution)/shard_map/ppermute | solution.py:22
  79.6 6.0 %collective-permute-start.11 = (f32[6,1,256]{2,1,0:T(1,128)S(1)}, f32[6,1,256]{2,1,0:T(1,128)S(1)}, u32[]{:S(2)}, u32[]{:S(2)}) collective-permute-start(f32[6,1,256]{2,1,0:T(1,128)S(1)} %get-tuple-element.61), channel_id=1, source_target_pairs={{1,0},{2,1},{3,2},{4,3},{5,4},{6,5},{7,6},{8,7},{9,8},{10,9},{11,1... | collective-permute-start | bytes 18440 | tf_op jit(solution)/shard_map/ppermute | solution.py:22
  89.5 6.3 %collective-permute-start.3 = (f32[10,1,512]{2,1,0:T(1,128)S(1)}, f32[10,1,512]{2,1,0:T(1,128)S(1)}, u32[]{:S(2)}, u32[]{:S(2)}) collective-permute-start(f32[10,1,512]{2,1,0:T(1,128)S(1)} %get-tuple-element.38), channel_id=1, source_target_pairs={{1,0},{2,1},{3,2},{4,3},{5,4},{6,5},{7,6},{8,7},{9,8},{10,9},{11,1... | collective-permute-start | bytes 61448 | tf_op jit(solution)/shard_map/ppermute | solution.py:22
  104.8 6.3 %collective-permute-start.6 = (f32[10,1,512]{2,1,0:T(1,128)S(1)}, f32[10,1,512]{2,1,0:T(1,128)S(1)}, u32[]{:S(2)}, u32[]{:S(2)}) collective-permute-start(f32[10,1,512]{2,1,0:T(1,128)S(1)} %get-tuple-element.35), channel_id=1, source_target_pairs={{1,0},{2,1},{3,2},{4,3},{5,4},{6,5},{7,6},{8,7},{9,8},{10,9},{11,1... | collective-permute-start | bytes 61448 | tf_op jit(solution)/shard_map/ppermute | solution.py:22
  113.1 5.8 %collective-permute-done.7 = f32[10,1,512]{2,1,0:T(1,128)S(1)} collective-permute-done((f32[10,1,512]{2,1,0:T(1,128)S(1)}, f32[10,1,512]{2,1,0:T(1,128)S(1)}, u32[]{:S(2)}, u32[]{:S(2)}) %collective-permute-start.7) | collective-permute-done | bytes 20512 | tf_op jit(solution)/shard_map/ppermute | solution.py:19
  128.5 3.9 collective-permute-start.15
  136.7 18.1 %reshape.218 = f32[4,2,8,2,256,2]{5,4,3,2,1,0:T(8,128)} reshape(f32[8,16,512]{2,1,0:T(8,128)S(1)} %fusion.30) | data formatting | bytes 524288 | tf_op jit(solution)/shard_map/reshape | solution.py:81
  154.8 7.0 %reduce_sum.69 = f32[4,8,256]{2,1,0:T(8,128)S(1)} reduce(f32[4,2,8,2,256,2]{5,4,3,2,1,0:T(8,128)} %reshape.218, f32[]{:T(128)} %constant.36.clone.1), dimensions={1,3,5}, to_apply=%region_1.2 | reduce | flops 57344 | bytes 294916 | tf_op jit(solution)/shard_map/reduce_sum | solution.py:81
  170.8 3.9 collective-permute-start.19
  187.4 4.1 collective-permute-start.27
  245.1 3.9 collective-permute-start.43
  262.2 3.9 collective-permute-start.47
  272.1 5.0 %all-to-all-start = ((f32[1,2,64]{1,0,2:T(1,128)}), f32[1,2,64]{1,0,2:T(1,128)S(1)}, u32[]{:S(2)}, u32[]{:S(2)}) async-start(f32[1,2,64]{1,0,2:T(1,128)} %bitcast.19), calls=%async_computation | async-start | bytes 65536 | tf_op jit(solution)/shard_map/all_to_all | solution.py:124
  277.2 8.6 %all-to-all-done = f32[1,2,64]{1,0,2:T(1,128)S(1)} async-done(((f32[1,2,64]{1,0,2:T(1,128)}), f32[1,2,64]{1,0,2:T(1,128)S(1)}, u32[]{:S(2)}, u32[]{:S(2)}) %all-to-all-start) | async-done | bytes 544 | tf_op jit(solution)/shard_map/all_to_all | solution.py:124
  288.3 4.9 %all-to-all-start.1 = ((f32[1,64,2]{2,0,1:T(1,128)}), f32[1,64,2]{2,0,1:T(1,128)S(1)}, u32[]{:S(2)}, u32[]{:S(2)}) async-start(f32[1,64,2]{2,0,1:T(1,128)} %copy.10), calls=%async_computation.1 | async-start | bytes 65536 | tf_op jit(solution)/shard_map/all_to_all | solution.py:126
  293.2 4.0 all-to-all-done.1
  299.3 7.7 %all_to_all.51 = f32[8,8,2]{1,2,0:T(2,128)S(1)} all-to-all(f32[8,8,2]{1,2,0:T(2,128)S(1)} %copy.13), channel_id=1, replica_groups=mesh['gx'=8,'gy'=32] {'gx'}, dimensions={0} | all-to-all | bytes 1024 | tf_op jit(solution)/shard_map/all_to_all | solution.py:135
  308.1 12.9 %all_to_all.52 = f32[1,64,2]{2,0,1:T(1,128)S(1)} all-to-all(f32[1,64,2]{2,0,1:T(1,128)S(1)} %copy.15), channel_id=1, replica_groups=mesh['gx'=8,'gy'=32] {'gy'}, dimensions={1} | all-to-all | bytes 1024 | tf_op jit(solution)/shard_map/all_to_all | solution.py:137
  336.2 4.3 collective-permute-done.51
  432.7 6.5 %broadcast_in_dim.68 = f32[4,2,8,2,256,2]{5,4,3,2,1,0:T(8,128)} broadcast(f32[4,8,256]{2,1,0:T(8,128)S(1)} %fusion.57), dimensions={0,2,4} | broadcast | bytes 294912 | tf_op jit(solution)/shard_map/broadcast_in_dim | solution.py:86
  439.1 12.7 %reshape.225 = f32[8,16,512]{2,1,0:T(8,128)S(1)} reshape(f32[4,2,8,2,256,2]{5,4,3,2,1,0:T(8,128)} %broadcast_in_dim.68) | data formatting | bytes 524288 | tf_op jit(solution)/shard_map/reshape | solution.py:87
  (365 shorter events, 311.9 us)
Async XLA Ops:
  28.5 18.9 %collective-permute-start.32 = (f32[1,2,64]{2,1,0:T(2,128)S(1)}, f32[1,2,64]{2,1,0:T(2,128)S(1)}, u32[]{:S(2)}, u32[]{:S(2)}) collective-permute-start(f32[1,2,64]{2,1,0:T(2,128)S(1)} %multiply_bitcast_fusion), channel_id=1, source_target_pairs={{0,32},{32,64},{64,96},{96,128},{128,160},{160,192},{192,224},{1,3... | collective-permute-start | bytes 1544 | tf_op jit(solution)/shard_map/ppermute | solution.py:19
  30.5 17.0 %collective-permute-start.33 = (f32[1,2,64]{2,1,0:T(2,128)S(1)}, f32[1,2,64]{2,1,0:T(2,128)S(1)}, u32[]{:S(2)}, u32[]{:S(2)}) collective-permute-start(f32[1,2,64]{2,1,0:T(2,128)S(1)} %multiply_bitcast_fusion), channel_id=1, source_target_pairs={{32,0},{64,32},{96,64},{128,96},{160,128},{192,160},{224,192},{33,... | collective-permute-start | bytes 1544 | tf_op jit(solution)/shard_map/ppermute | solution.py:22
  34.1 52.9 %collective-permute-start = (f32[1,16,512]{2,1,0:T(8,128)S(1)}, f32[1,16,512]{2,1,0:T(8,128)S(1)}, u32[]{:S(2)}, u32[]{:S(2)}) collective-permute-start(f32[1,16,512]{2,1,0:T(8,128)S(1)} %get-tuple-element.51), channel_id=1, source_target_pairs={{0,32},{32,64},{64,96},{96,128},{128,160},{160,192},{192,224},{1,3... | collective-permute-start | bytes 98312 | tf_op jit(solution)/shard_map/ppermute | solution.py:19
  36.1 51.1 %collective-permute-start.1 = (f32[1,16,512]{2,1,0:T(8,128)S(1)}, f32[1,16,512]{2,1,0:T(8,128)S(1)}, u32[]{:S(2)}, u32[]{:S(2)}) collective-permute-start(f32[1,16,512]{2,1,0:T(8,128)S(1)} %get-tuple-element.50), channel_id=1, source_target_pairs={{32,0},{64,32},{96,64},{128,96},{160,128},{192,160},{224,192},{33,... | collective-permute-start | bytes 98312 | tf_op jit(solution)/shard_map/ppermute | solution.py:22
  39.7 37.2 %collective-permute-start.8 = (f32[1,8,256]{2,1,0:T(8,128)S(1)}, f32[1,8,256]{2,1,0:T(8,128)S(1)}, u32[]{:S(2)}, u32[]{:S(2)}) collective-permute-start(f32[1,8,256]{2,1,0:T(8,128)S(1)} %get-tuple-element.70), channel_id=1, source_target_pairs={{0,32},{32,64},{64,96},{96,128},{128,160},{160,192},{192,224},{1,3... | collective-permute-start | bytes 24584 | tf_op jit(solution)/shard_map/ppermute | solution.py:19
  47.5 10.3 %collective-permute-start.34 = (f32[3,1,64]{2,1,0:T(1,128)S(1)}, f32[3,1,64]{2,1,0:T(1,128)S(1)}, u32[]{:S(2)}, u32[]{:S(2)}) collective-permute-start(f32[3,1,64]{2,1,0:T(1,128)S(1)} %get-tuple-element.106), channel_id=1, source_target_pairs={{0,1},{1,2},{2,3},{3,4},{4,5},{5,6},{6,7},{7,8},{8,9},{9,10},{10,1... | collective-permute-start | bytes 2312 | tf_op jit(solution)/shard_map/ppermute | solution.py:19
  51.4 9.8 %collective-permute-start.35 = (f32[3,1,64]{2,1,0:T(1,128)S(1)}, f32[3,1,64]{2,1,0:T(1,128)S(1)}, u32[]{:S(2)}, u32[]{:S(2)}) collective-permute-start(f32[3,1,64]{2,1,0:T(1,128)S(1)} %get-tuple-element.107), channel_id=1, source_target_pairs={{1,0},{2,1},{3,2},{4,3},{5,4},{6,5},{7,6},{8,7},{9,8},{10,9},{11,1... | collective-permute-start | bytes 2312 | tf_op jit(solution)/shard_map/ppermute | solution.py:22
  64.7 8.6 %collective-permute-start.22 = (f32[4,1,128]{2,1,0:T(1,128)S(1)}, f32[4,1,128]{2,1,0:T(1,128)S(1)}, u32[]{:S(2)}, u32[]{:S(2)}) collective-permute-start(f32[4,1,128]{2,1,0:T(1,128)S(1)} %get-tuple-element.84), channel_id=1, source_target_pairs={{0,1},{1,2},{2,3},{3,4},{4,5},{5,6},{6,7},{7,8},{8,9},{9,10},{10,1... | collective-permute-start | bytes 6152 | tf_op jit(solution)/shard_map/ppermute | solution.py:19
  66.6 9.7 %collective-permute-start.23 = (f32[4,1,128]{2,1,0:T(1,128)S(1)}, f32[4,1,128]{2,1,0:T(1,128)S(1)}, u32[]{:S(2)}, u32[]{:S(2)}) collective-permute-start(f32[4,1,128]{2,1,0:T(1,128)S(1)} %get-tuple-element.85), channel_id=1, source_target_pairs={{1,0},{2,1},{3,2},{4,3},{5,4},{6,5},{7,6},{8,7},{9,8},{10,9},{11,1... | collective-permute-start | bytes 6152 | tf_op jit(solution)/shard_map/ppermute | solution.py:22
  77.7 8.0 %collective-permute-start.10 = (f32[6,1,256]{2,1,0:T(1,128)S(1)}, f32[6,1,256]{2,1,0:T(1,128)S(1)}, u32[]{:S(2)}, u32[]{:S(2)}) collective-permute-start(f32[6,1,256]{2,1,0:T(1,128)S(1)} %get-tuple-element.60), channel_id=1, source_target_pairs={{0,1},{1,2},{2,3},{3,4},{4,5},{5,6},{6,7},{7,8},{8,9},{9,10},{10,1... | collective-permute-start | bytes 18440 | tf_op jit(solution)/shard_map/ppermute | solution.py:19
  87.6 8.3 %collective-permute-start.2 = (f32[10,1,512]{2,1,0:T(1,128)S(1)}, f32[10,1,512]{2,1,0:T(1,128)S(1)}, u32[]{:S(2)}, u32[]{:S(2)}) collective-permute-start(f32[10,1,512]{2,1,0:T(1,128)S(1)} %get-tuple-element.37), channel_id=1, source_target_pairs={{0,1},{1,2},{2,3},{3,4},{4,5},{5,6},{6,7},{7,8},{8,9},{9,10},{10,1... | collective-permute-start | bytes 61448 | tf_op jit(solution)/shard_map/ppermute | solution.py:19
  89.5 7.8 %collective-permute-start.3 = (f32[10,1,512]{2,1,0:T(1,128)S(1)}, f32[10,1,512]{2,1,0:T(1,128)S(1)}, u32[]{:S(2)}, u32[]{:S(2)}) collective-permute-start(f32[10,1,512]{2,1,0:T(1,128)S(1)} %get-tuple-element.38), channel_id=1, source_target_pairs={{1,0},{2,1},{3,2},{4,3},{5,4},{6,5},{7,6},{8,7},{9,8},{10,9},{11,1... | collective-permute-start | bytes 61448 | tf_op jit(solution)/shard_map/ppermute | solution.py:22
  104.8 8.3 %collective-permute-start.6 = (f32[10,1,512]{2,1,0:T(1,128)S(1)}, f32[10,1,512]{2,1,0:T(1,128)S(1)}, u32[]{:S(2)}, u32[]{:S(2)}) collective-permute-start(f32[10,1,512]{2,1,0:T(1,128)S(1)} %get-tuple-element.35), channel_id=1, source_target_pairs={{1,0},{2,1},{3,2},{4,3},{5,4},{6,5},{7,6},{8,7},{9,8},{10,9},{11,1... | collective-permute-start | bytes 61448 | tf_op jit(solution)/shard_map/ppermute | solution.py:22
  111.1 7.8 %collective-permute-start.7 = (f32[10,1,512]{2,1,0:T(1,128)S(1)}, f32[10,1,512]{2,1,0:T(1,128)S(1)}, u32[]{:S(2)}, u32[]{:S(2)}) collective-permute-start(f32[10,1,512]{2,1,0:T(1,128)S(1)} %get-tuple-element.36), channel_id=1, source_target_pairs={{0,1},{1,2},{2,3},{3,4},{4,5},{5,6},{6,7},{7,8},{8,9},{9,10},{10,1... | collective-permute-start | bytes 61448 | tf_op jit(solution)/shard_map/ppermute | solution.py:19
  128.5 7.8 %collective-permute-start.15 = (f32[10,1,512]{2,1,0:T(1,128)S(1)}, f32[10,1,512]{2,1,0:T(1,128)S(1)}, u32[]{:S(2)}, u32[]{:S(2)}) collective-permute-start(f32[10,1,512]{2,1,0:T(1,128)S(1)} %get-tuple-element.34), channel_id=1, source_target_pairs={{0,1},{1,2},{2,3},{3,4},{4,5},{5,6},{6,7},{7,8},{8,9},{9,10},{10,1... | collective-permute-start | bytes 61448 | tf_op jit(solution)/shard_map/ppermute | solution.py:19
  170.8 7.6 %collective-permute-start.19 = (f32[6,1,256]{2,1,0:T(1,128)S(1)}, f32[6,1,256]{2,1,0:T(1,128)S(1)}, u32[]{:S(2)}, u32[]{:S(2)}) collective-permute-start(f32[6,1,256]{2,1,0:T(1,128)S(1)} %get-tuple-element.59), channel_id=1, source_target_pairs={{0,1},{1,2},{2,3},{3,4},{4,5},{5,6},{6,7},{7,8},{8,9},{9,10},{10,1... | collective-permute-start | bytes 18440 | tf_op jit(solution)/shard_map/ppermute | solution.py:19
  187.4 7.6 %collective-permute-start.27 = (f32[6,1,256]{2,1,0:T(1,128)S(1)}, f32[6,1,256]{2,1,0:T(1,128)S(1)}, u32[]{:S(2)}, u32[]{:S(2)}) collective-permute-start(f32[6,1,256]{2,1,0:T(1,128)S(1)} %get-tuple-element.57), channel_id=1, source_target_pairs={{0,1},{1,2},{2,3},{3,4},{4,5},{5,6},{6,7},{7,8},{8,9},{9,10},{10,1... | collective-permute-start | bytes 18440 | tf_op jit(solution)/shard_map/ppermute | solution.py:19
  209.1 7.6 %collective-permute-start.31 = (f32[4,1,128]{2,1,0:T(1,128)S(1)}, f32[4,1,128]{2,1,0:T(1,128)S(1)}, u32[]{:S(2)}, u32[]{:S(2)}) collective-permute-start(f32[4,1,128]{2,1,0:T(1,128)S(1)} %get-tuple-element.83), channel_id=1, source_target_pairs={{0,1},{1,2},{2,3},{3,4},{4,5},{5,6},{6,7},{7,8},{8,9},{9,10},{10,1... | collective-permute-start | bytes 6152 | tf_op jit(solution)/shard_map/ppermute | solution.py:19
  272.1 13.7 %all-to-all-start = ((f32[1,2,64]{1,0,2:T(1,128)}), f32[1,2,64]{1,0,2:T(1,128)S(1)}, u32[]{:S(2)}, u32[]{:S(2)}) async-start(f32[1,2,64]{1,0,2:T(1,128)} %bitcast.19), calls=%async_computation | async-start | bytes 65536 | tf_op jit(solution)/shard_map/all_to_all | solution.py:124
  288.3 8.9 %all-to-all-start.1 = ((f32[1,64,2]{2,0,1:T(1,128)}), f32[1,64,2]{2,0,1:T(1,128)S(1)}, u32[]{:S(2)}, u32[]{:S(2)}) async-start(f32[1,64,2]{2,0,1:T(1,128)} %copy.10), calls=%async_computation.1 | async-start | bytes 65536 | tf_op jit(solution)/shard_map/all_to_all | solution.py:126
  405.3 7.6 %collective-permute-start.67 = (f32[6,1,256]{2,1,0:T(1,128)S(1)}, f32[6,1,256]{2,1,0:T(1,128)S(1)}, u32[]{:S(2)}, u32[]{:S(2)}) collective-permute-start(f32[6,1,256]{2,1,0:T(1,128)S(1)} %get-tuple-element.55), channel_id=1, source_target_pairs={{0,1},{1,2},{2,3},{3,4},{4,5},{5,6},{6,7},{7,8},{8,9},{9,10},{10,1... | collective-permute-start | bytes 18440 | tf_op jit(solution)/shard_map/ppermute | solution.py:19
  423.4 7.6 %collective-permute-start.71 = (f32[6,1,256]{2,1,0:T(1,128)S(1)}, f32[6,1,256]{2,1,0:T(1,128)S(1)}, u32[]{:S(2)}, u32[]{:S(2)}) collective-permute-start(f32[6,1,256]{2,1,0:T(1,128)S(1)} %get-tuple-element.53), channel_id=1, source_target_pairs={{0,1},{1,2},{2,3},{3,4},{4,5},{5,6},{6,7},{7,8},{8,9},{9,10},{10,1... | collective-permute-start | bytes 18440 | tf_op jit(solution)/shard_map/ppermute | solution.py:19
  461.0 7.8 %collective-permute-start.75 = (f32[10,1,512]{2,1,0:T(1,128)S(1)}, f32[10,1,512]{2,1,0:T(1,128)S(1)}, u32[]{:S(2)}, u32[]{:S(2)}) collective-permute-start(f32[10,1,512]{2,1,0:T(1,128)S(1)} %get-tuple-element.32), channel_id=1, source_target_pairs={{0,1},{1,2},{2,3},{3,4},{4,5},{5,6},{6,7},{7,8},{8,9},{9,10},{10,1... | collective-permute-start | bytes 61448 | tf_op jit(solution)/shard_map/ppermute | solution.py:19
  478.4 7.8 %collective-permute-start.79 = (f32[10,1,512]{2,1,0:T(1,128)S(1)}, f32[10,1,512]{2,1,0:T(1,128)S(1)}, u32[]{:S(2)}, u32[]{:S(2)}) collective-permute-start(f32[10,1,512]{2,1,0:T(1,128)S(1)} %get-tuple-element.30), channel_id=1, source_target_pairs={{0,1},{1,2},{2,3},{3,4},{4,5},{5,6},{6,7},{7,8},{8,9},{9,10},{10,1... | collective-permute-start | bytes 61448 | tf_op jit(solution)/shard_map/ppermute | solution.py:19
  (82 other events, 1181.4 us)
where the time goes:
time: 491 us; the launch traced here: 487 us
  starting transfers between devices  231 us (47%)
  waiting for transfers between devices  111 us (23%)
  local copies, waits for them, and re-layouts  66.9 us (14%)
  other arithmetic  49.5 us (10%)
  blocking collectives  20.6 us (4%)
  matrix products  6.58 us (1%)
    ppermute x40, starting transfers between devices, with_halo(): lax.ppermute(lax.slice_in_dim(block, block.shape[dim] - width, None, axis...  117 us
    ppermute x40, starting transfers between devices, with_halo(): lax.ppermute(lax.slice_in_dim(block, 0, width, axis=dim), axis, backward)  104 us
    ppermute x40, waiting for transfers between devices, with_halo(): lax.ppermute(lax.slice_in_dim(block, block.shape[dim] - width, None, axis...  94.7 us
    reshape x3, local copies, waits for them, and re-layouts, restrict(): values.reshape(nx // 2, 2, ny // 2, 2, nz // 2, 2).mean(axis=(1, 3, 5))  39.9 us
    reduce_sum x8, other arithmetic, restrict(): values.reshape(nx // 2, 2, ny // 2, 2, nz // 2, 2).mean(axis=(1, 3, 5))  15.3 us
    reshape x2, local copies, waits for them, and re-layouts, prolong(): return grown.reshape(2 * nx, 2 * ny, 2 * nz)  14.5 us
    all_to_all x1, blocking collectives, coarse_solve(): lax.all_to_all(coeffs, 'gy', split_axis=1, concat_axis=2, tiled=True)  12.9 us
  transfers between devices with their start and end apart: 82, of which 38 were waited for; matrix products, arithmetic and copies ran while one was open for 4% of the time, Pallas kernels for 0%

commit v1 on v0

v1 whole, which is shorter than its diff:
```python
import math
import numpy as np
import jax
import jax.numpy as jnp
from jax import lax
from jax.experimental import pallas as pl
from jax.experimental.pallas import tpu as pltpu
from jax.sharding import PartitionSpec as P

MESH = pl.DeviceIdType.MESH
F32 = jnp.float32
THETA = 1.25
DELTA = 0.75
SIGMA = THETA / DELTA
RHO0 = 1.0 / SIGMA
RHO1 = 1.0 / (2.0 * SIGMA - RHO0)
C_FIRST = 1.0 / THETA
C_OLD = RHO1 * RHO0
C_NEW = 2.0 * RHO1 / DELTA
GX, GY = 8, 32
NEIGHBOURS = [(a, b) for a in (-1, 0, 1) for b in (-1, 0, 1) if (a, b) != (0, 0)]
BRICKS = [(a, b) for a in range(GX) for b in (-1, 0, 1) if (a, b) != (0, 0)]
LINE = [(0, b) for b in range(1, GY)]
PEERS = list(
    dict.fromkeys((a % GX, b % GY) for a, b in NEIGHBOURS + BRICKS + LINE)
)


def dct_matrix(count):
    wave = np.arange(count)[:, None].astype(np.float64)
    place = np.arange(count)[None, :].astype(np.float64)
    norms = np.where(wave == 0, math.sqrt(1.0 / count), math.sqrt(2.0 / count))
    return norms * np.cos(np.pi * wave * (2 * place + 1) / (2 * count))


def constants():
    cx, cy, cz = dct_matrix(8), dct_matrix(64), dct_matrix(64)
    forward = np.einsum("ax,cz->xzac", cx, cz).reshape(512, 512)
    turned = np.stack([np.roll(cy, 32 - 2 * g, axis=1) for g in range(GY)])
    window = np.stack([t.T[24:40] for t in turned])
    lam = [2 - 2 * np.cos(np.pi * np.arange(n) / n) for n in (8, 64, 64)]
    total = (lam[1][:, None, None] + lam[0][None, :, None] + lam[2][None, None, :]) * 4.0**-3
    total[0, 0, 0] = 1.0
    table = 1.0 / total
    table[0, 0, 0] = 0.0
    pair = np.zeros((256, 128))
    pair[np.arange(256), np.arange(256) // 2] = 0.125
    grow = np.zeros((128, 256))
    grow[np.arange(256) // 2, np.arange(256)] = 1.0
    rows = np.zeros((72, 16))
    for j in range(24):
        if 2 <= j < 22:
            rows[j, (j + 4) // 2] = 1.0
    for j in range(16):
        rows[24 + j, 2 + j // 2] = 1.0
    for j in range(12):
        rows[40 + j, 6 + j // 2] = 1.0
    for j in range(8):
        rows[56 + j, 2 * j] = 1.0
        rows[56 + j, 2 * j + 1] = 1.0
    for j in range(2):
        rows[64 + j, 4 + 2 * j] = 1.0
        rows[64 + j, 5 + 2 * j] = 1.0
    out = (forward, forward.T, turned, window, table.reshape(64, 512), pair, grow, rows)
    return tuple(np.ascontiguousarray(v, dtype=np.float32) for v in out)


def device(offset):
    gx, gy = lax.axis_index("gx"), lax.axis_index("gy")
    return (lax.rem(gx + (offset[0] % GX), GX), lax.rem(gy + (offset[1] % GY), GY))


def recip(value):
    guess = pl.reciprocal(value, approx=True)
    return guess * (2.0 - value * guess)


def harm(a, b):
    return (a * b) * recip(a + b)


def up(value, axis, step=1):
    return pltpu.roll(value, value.shape[axis] - step, axis)


def down(value, axis, step=1):
    return pltpu.roll(value, step, axis)


def dot(a, b):
    return jnp.dot(a, b, precision=lax.Precision.HIGHEST, preferred_element_type=F32)


def iota(shape, axis):
    return lax.broadcasted_iota(jnp.int32, shape, axis)


def halo_copies(ref, at, size, halo, send, recv):
    copies = []
    for a, b in NEIGHBOURS:
        take, put = [], []
        for side, s0, n, h in zip((a, b), at, size, halo):
            if side == 0:
                take.append((s0, n))
                put.append(s0)
            elif side > 0:
                take.append((s0 + n - h, h))
                put.append(s0 - h)
            else:
                take.append((s0, h))
                put.append(s0 + n)
        (x_from, x_count), (y_from, y_count) = take
        if b == 0:
            ends = [y_from] + list(range(y_from + 4, y_from + y_count, 8)) + [y_from + y_count]
        else:
            ends = [y_from, y_from + y_count]
        for low, high in zip(ends[:-1], ends[1:]):
            k = len(copies)
            copies.append(
                pltpu.make_async_remote_copy(
                    ref.at[pl.ds(x_from, x_count), pl.ds(low, high - low), :],
                    ref.at[pl.ds(put[0], x_count), pl.ds(put[1] + low - y_from, high - low), :],
                    send.at[k],
                    recv.at[k],
                    device_id=device((a, b)),
                    device_id_type=MESH,
                )
            )
    return copies


def start(copies):
    for c in copies:
        c.start()


def arrive(copies):
    for c in copies:
        c.wait_recv()


def sent(copies):
    for c in copies:
        c.wait_send()


def planes_op(v, wx, wy, wz, lo, hi):
    c = v[lo:hi]
    fx = wx[lo - 1 : hi] * (v[lo : hi + 1] - v[lo - 1 : hi])
    fy = wy[lo:hi] * (up(c, 1) - c)
    fz = wz[lo:hi] * (up(c, 2) - c)
    return (fx[1:] - fx[:-1]) + (fy - down(fy, 1)) + (fz - down(fz, 2))


def ring_op(v, wx, wy, wz):
    fx = wx * (jnp.concatenate([v[1:], v[:1]]) - v)
    fy = wy * (up(v, 1) - v)
    fz = wz * (up(v, 2) - v)
    fx = fx - jnp.concatenate([fx[-1:], fx[:-1]])
    return fx + (fy - down(fy, 1)) + (fz - down(fz, 2))


def flat_op(v, wx, wy, wz):
    fx = wx * (up(v, 1, 64) - v)
    fy = wy * (up(v, 0) - v)
    fz = wz * (up(v, 1) - v)
    return (fx - down(fx, 1, 64)) + (fy - down(fy, 0)) + (fz - down(fz, 1))


def kernel(
    r_in, b_in, fwd_in, inv_in, turn_in, wind_in, table_in, pair, grow, rows, out,
    b0, r0, wx0, wy0, wz0, g0, d0, e0, q0, xp0, y0,
    b1, r1, xp1, b2, r2, xp2, e2, m2, b3, r3, m3,
    fwd, inv, turn, wind, table,
    local, halo_s, halo_r, many_s, many_r,
):
    gx, gy = lax.axis_index("gx"), lax.axis_index("gy")
    own = [
        pltpu.make_async_copy(
            src.at[:, pl.ds(4 * j, 4), :],
            dst.at[pl.ds(3, 8), pl.ds(4 + 4 * j, 4), :],
            local.at[k, j],
        )
        for k, (src, dst) in enumerate(((b_in, b0), (r_in, r0)))
        for j in range(4)
    ]
    fixed = [
        pltpu.make_async_copy(fwd_in, fwd, local.at[2, 0]),
        pltpu.make_async_copy(inv_in, inv, local.at[2, 1]),
        pltpu.make_async_copy(turn_in.at[gy], turn, local.at[2, 2]),
        pltpu.make_async_copy(wind_in.at[gy], wind, local.at[2, 3]),
        pltpu.make_async_copy(table_in, table, local.at[3, 0]),
    ]
    start(own + fixed)
    barrier = pltpu.get_barrier_semaphore()
    for p in PEERS:
        pl.semaphore_signal(barrier, inc=1, device_id=device(p), device_id_type=MESH)

    down0 = rows[56:64, :]
    down2 = rows[64:72, :]

    for c in own[:4]:
        c.wait()
    flat = []
    for i in range(4):
        s = b0[3 + 2 * i, 4:20, :] + b0[4 + 2 * i, 4:20, :]
        flat.append(dot(down0, s))
    flat = jnp.concatenate(flat, axis=0)
    flat = jnp.concatenate([dot(flat[:, :256], pair[...]), dot(flat[:, 256:], pair[...])], axis=1)
    for i in range(4):
        b1[3 + i, 4:12, :] = flat[8 * i : 8 * i + 8]
    half = rows[56:60, 0:8]
    for i in range(2):
        s = flat[16 * i : 16 * i + 8] + flat[16 * i + 8 : 16 * i + 16]
        s = dot(dot(half, s), pair[...])
        b2[2 * gx + i, 4:8, :] = s

    for c in own[4:]:
        c.wait()
    pl.semaphore_wait(barrier, len(PEERS))

    b0_out = halo_copies(b0, (3, 4), (8, 16), (3, 3), halo_s.at[0], halo_r.at[0])
    r0_out = halo_copies(r0, (3, 4), (8, 16), (2, 2), halo_s.at[1], halo_r.at[1])
    b1_out = halo_copies(b1, (3, 4), (4, 8), (3, 4), halo_s.at[2], halo_r.at[2])
    r1_out = halo_copies(r1, (3, 4), (4, 8), (2, 2), halo_s.at[3], halo_r.at[3])
    xp0_out = halo_copies(xp0, (3, 4), (8, 16), (2, 2), halo_s.at[4], halo_r.at[4])
    xp1_out = halo_copies(xp1, (3, 4), (4, 8), (3, 3), halo_s.at[5], halo_r.at[5])
    start(b0_out)
    start(r0_out)
    start(b1_out)

    def bricks(ref, k):
        for a, b in BRICKS:
            pltpu.make_async_remote_copy(
                ref.at[pl.ds(2 * gx, 2), pl.ds(4, 4), :],
                ref.at[pl.ds(2 * gx, 2), pl.ds(4 - 4 * b, 4), :],
                many_s.at[k],
                many_r.at[k],
                device_id=device((a, b)),
                device_id_type=MESH,
            ).start()

    def lines(ref, k):
        for _, b in LINE:
            pltpu.make_async_remote_copy(
                ref.at[pl.ds(32, 2), :],
                ref.at[pl.ds((32 - 2 * b) % 64, 2), :],
                many_s.at[k],
                many_r.at[k],
                device_id=device((0, b)),
                device_id_type=MESH,
            ).start()

    def all_of(ref, k):
        return pltpu.make_async_remote_copy(
            ref, ref, many_s.at[k], many_r.at[k], device_id=device((0, 1)), device_id_type=MESH
        )

    bricks(b2, 0)
    arrive(b0_out)
    arrive(r0_out)

    row = iota((24, 512), 0)
    lane = iota((24, 512), 1)
    edge = jnp.where(gy == GY - 1, 19, jnp.where(gy == 0, 3, -1))
    mul_y = jnp.where(row == edge, 0.0, 2.0)
    mul_z = jnp.where(lane == 511, 0.0, 2.0)
    cut0 = jnp.where(gx == GX - 1, 10, jnp.where(gx == 0, 2, -1))

    wx0[0] = 2.0 * harm(b0[0], b0[1])

    @pl.loop(1, 13)
    def _(i):
        c = b0[i]
        wx = harm(c, b0[i + 1]) * jnp.where(i == cut0, 0.0, 2.0)
        wy = harm(c, up(c, 0)) * mul_y
        wz = harm(c, up(c, 1)) * mul_z
        wx0[i] = wx
        wy0[i] = wy
        wz0[i] = wz
        g = recip((wx + wx0[i - 1]) + (wy + down(wy, 0)) + (wz + down(wz, 1)))
        g0[i] = g
        d0[i] = g * r0[i] * C_FIRST

    def op0(ref, i):
        c = ref[i]
        fy = wy0[i] * (up(c, 0) - c)
        fz = wz0[i] * (up(c, 1) - c)
        fx = wx0[i] * (ref[i + 1] - c) - wx0[i - 1] * (c - ref[i - 1])
        return fx + (fy - down(fy, 0)) + (fz - down(fz, 1))

    @pl.loop(2, 12)
    def _(i):
        q = r0[i] + op0(d0, i)
        q0[i] = q
        e0[i] = C_OLD * d0[i] + C_NEW * (g0[i] * q)

    @pl.loop(3, 11)
    def _(i):
        q = q0[i] + op0(e0, i)
        q0[i] = q
        x = d0[i] + e0[i]
        xp0[i, 4:20, :] = x[4:20]

    flat = []
    for i in range(4):
        s = q0[3 + 2 * i, 4:20, :] + q0[4 + 2 * i, 4:20, :]
        flat.append(dot(down0, s))
    flat = jnp.concatenate(flat, axis=0)
    flat = jnp.concatenate([dot(flat[:, :256], pair[...]), dot(flat[:, 256:], pair[...])], axis=1)
    for i in range(4):
        r1[3 + i, 4:12, :] = flat[8 * i : 8 * i + 8]
    start(r1_out)
    start(xp0_out)

    arrive(b1_out)
    v = b1[...]
    shape = (10, 16, 256)
    edge = jnp.where(gy == GY - 1, 11, jnp.where(gy == 0, 3, -1))
    cut = jnp.where(gx == GX - 1, 6, jnp.where(gx == 0, 2, -1))
    keep_x = jnp.where(iota((9, 16, 256), 0) == cut, 0.0, 0.5)
    wx1 = harm(v[:-1], v[1:]) * keep_x
    wy1 = harm(v, up(v, 1)) * jnp.where(iota(shape, 1) == edge, 0.0, 0.5)
    wz1 = harm(v, up(v, 2)) * jnp.where(iota(shape, 2) == 255, 0.0, 0.5)
    c = slice(1, 9)
    g1 = recip(
        (wx1[1:] + wx1[:-1]) + (wy1[c] + down(wy1[c], 1)) + (wz1[c] + down(wz1[c], 2))
    )

    all_of(m2, 0).wait_recv()

    def to_flat(value):
        value = jnp.where(iota((16, 16, 128), 1) < 8, value, 0.0)
        parts = []
        for t in range(4):
            s = jnp.concatenate(
                [value[4 * t] + value[4 * t + 1], value[4 * t + 2] + value[4 * t + 3]], axis=1
            )
            parts.append(dot(s, pair[...]))
        return dot(down2, jnp.concatenate(parts, axis=1))[0:2]

    v = b2[...]
    b3[32:34, :] = to_flat(v)
    lines(b3, 2)
    shape = (16, 16, 128)
    edge = jnp.where(gy == GY - 1, 7, jnp.where(gy == 0, 3, -1))
    scale = 2.0 * 4.0**-2
    wx2 = harm(v, jnp.concatenate([v[1:], v[:1]])) * jnp.where(iota(shape, 0) == 15, 0.0, scale)
    wy2 = harm(v, up(v, 1)) * jnp.where(iota(shape, 1) == edge, 0.0, scale)
    wz2 = harm(v, up(v, 2)) * jnp.where(iota(shape, 2) == 127, 0.0, scale)
    g2 = recip(
        (wx2 + jnp.concatenate([wx2[-1:], wx2[:-1]]))
        + (wy2 + down(wy2, 1))
        + (wz2 + down(wz2, 2))
    )

    arrive(r1_out)
    f1 = r1[...]
    d = g1 * f1[1:9] * C_FIRST
    q = f1[2:8] + planes_op(d, wx1[1:8], wy1[1:9], wz1[1:9], 1, 7)
    e = C_OLD * d[1:7] + C_NEW * (g1[1:7] * q)
    q = q[1:5] + planes_op(e, wx1[2:7], wy1[2:8], wz1[2:8], 1, 5)
    xp1[3:7, 4:12, :] = (d[2:6] + e[1:5])[:, 4:12, :]
    for i in range(2):
        s = (q[2 * i] + q[2 * i + 1])[4:12]
        s = dot(dot(half, s), pair[...])
        r2[2 * gx + i, 4:8, :] = s
    bricks(r2, 1)
    start(xp1_out)

    all_of(m3, 2).wait_recv()
    v = b3[...]
    shape = (64, 512)
    scale = 2.0 * 4.0**-3
    lane = iota(shape, 1)
    edge = lax.rem(95 - 2 * gy, 64)
    wx3 = harm(v, up(v, 1, 64)) * jnp.where(lane >= 448, 0.0, scale)
    wy3 = harm(v, up(v, 0)) * jnp.where(iota(shape, 0) == edge, 0.0, scale)
    wz3 = harm(v, up(v, 1)) * jnp.where(lax.rem(lane, 64) == 63, 0.0, scale)
    g3 = recip((wx3 + down(wx3, 1, 64)) + (wy3 + down(wy3, 0)) + (wz3 + down(wz3, 1)))

    all_of(m2, 1).wait_recv()
    f2 = r2[...]
    d = g2 * f2 * C_FIRST
    q = f2 + ring_op(d, wx2, wy2, wz2)
    e = C_OLD * d + C_NEW * (g2 * q)
    q = q + ring_op(e, wx2, wy2, wz2)
    xp2[:, 4:8, :] = (d + e)[:, 4:8, :]
    q = jnp.where(iota((16, 16, 128), 1) >= 4, q, 0.0)
    r3[32:34, :] = to_flat(q)
    lines(r3, 3)
    xp2_out = [
        pltpu.make_async_remote_copy(
            xp2.at[:, pl.ds(4, 4), :],
            xp2.at[:, pl.ds(4 - 4 * b, 4), :],
            halo_s.at[6, k],
            halo_r.at[6, k],
            device_id=device((0, b)),
            device_id_type=MESH,
        )
        for k, b in enumerate((-1, 1))
    ]
    start(xp2_out)

    for c in fixed:
        c.wait()
    all_of(m3, 3).wait_recv()
    f3 = r3[...]
    d = g3 * f3 * C_FIRST
    q = f3 + flat_op(d, wx3, wy3, wz3)
    e = C_OLD * d + C_NEW * (g3 * q)
    q = q + flat_op(e, wx3, wy3, wz3)
    t = dot(dot(turn[...], q), fwd[...]) * table[...]
    t = dot(dot(wind[...], t), inv[...])
    w = slice(24, 40)
    x = d[w] + e[w] + t
    w3 = (wx3[w], wy3[w], wz3[w])
    q = f3[w] + flat_op(x, *w3)
    d = g3[w] * q * C_FIRST
    q = q + flat_op(d, *w3)
    x = x + d + (C_OLD * d + C_NEW * (g3[w] * q))

    x = dot(rows[40:56, :], x)
    wide = [dot(x[:, 128 * t : 128 * t + 128], grow[...]) for t in range(4)]
    wide = jnp.stack([wide[i // 4][:, 128 * (i // 2 % 2) : 128 * (i // 2 % 2) + 128] for i in range(16)])
    arrive(xp2_out)
    x = xp2[...] + wide
    q = f2 + ring_op(x, wx2, wy2, wz2)
    d = g2 * q * C_FIRST
    q = q + ring_op(d, wx2, wy2, wz2)
    x = x + d + (C_OLD * d + C_NEW * (g2 * q))
    line = iota((16, 16, 128), 1)
    x = jnp.where((line >= 2) & (line < 10), x, 0.0)
    e2[2:18] = x
    e2[0:2] = x[14:16]
    e2[18:20] = x[0:2]

    wide = [dot(rows[24:40, :], dot(e2[2 * gx + i], grow[...])) for i in range(6)]
    wide = jnp.stack([wide[(i + 1) // 2] for i in range(10)])
    arrive(xp1_out)
    x = xp1[...] + wide
    q = f1[1:9] + planes_op(x, wx1, wy1, wz1, 1, 9)
    d = g1 * q * C_FIRST
    q = q[1:7] + planes_op(d, wx1[1:8], wy1[1:9], wz1[1:9], 1, 7)
    x = x[2:8] + d[1:7] + (C_OLD * d[1:7] + C_NEW * (g1[1:7] * q))
    line = iota((6, 16, 256), 1)
    x = jnp.where((line >= 3) & (line < 13), x, 0.0)

    for i in range(6):
        s = dot(rows[0:24, :], x[i])
        y0[i] = jnp.concatenate([dot(s[:, :128], grow[...]), dot(s[:, 128:], grow[...])], axis=1)
    arrive(xp0_out)

    @pl.loop(1, 13)
    def _(i):
        e0[i] = xp0[i] + y0[(i + 3) // 2 - 2]

    @pl.loop(2, 12)
    def _(i):
        q = r0[i] + op0(e0, i)
        q0[i] = q
        d0[i] = g0[i] * q * C_FIRST

    @pl.loop(3, 11)
    def _(i):
        q = q0[i] + op0(d0, i)
        d = d0[i]
        x = e0[i] + d + (C_OLD * d + C_NEW * (g0[i] * q))
        out[i - 3] = x[4:20]

    sent(b0_out + r0_out + b1_out + r1_out + xp0_out + xp1_out + xp2_out)
    all_of(m2, 0).wait_send()
    all_of(m2, 1).wait_send()
    all_of(m3, 2).wait_send()
    all_of(m3, 3).wait_send()


def local(right_side, inverse_density):
    consts = constants()
    any_spec = pl.BlockSpec(memory_space=pl.ANY)
    vmem_spec = pl.BlockSpec(memory_space=pltpu.VMEM)
    fine = pltpu.VMEM((14, 24, 512), F32)
    scratch = [fine] * 10 + [
        pltpu.VMEM((6, 24, 512), F32),
        pltpu.VMEM((10, 16, 256), F32),
        pltpu.VMEM((10, 16, 256), F32),
        pltpu.VMEM((10, 16, 256), F32),
        pltpu.VMEM((16, 16, 128), F32),
        pltpu.VMEM((16, 16, 128), F32),
        pltpu.VMEM((16, 16, 128), F32),
        pltpu.VMEM((20, 16, 128), F32),
        pltpu.VMEM((len(BRICKS), 8, 128), F32),
        pltpu.VMEM((64, 512), F32),
        pltpu.VMEM((64, 512), F32),
        pltpu.VMEM((len(LINE), 8, 128), F32),
        pltpu.VMEM((512, 512), F32),
        pltpu.VMEM((512, 512), F32),
        pltpu.VMEM((64, 64), F32),
        pltpu.VMEM((16, 64), F32),
        pltpu.VMEM((64, 512), F32),
        pltpu.SemaphoreType.DMA((4, 4)),
        pltpu.SemaphoreType.DMA((7, 12)),
        pltpu.SemaphoreType.DMA((7, 12)),
        pltpu.SemaphoreType.DMA((4,)),
        pltpu.SemaphoreType.DMA((4,)),
    ]
    return pl.pallas_call(
        kernel,
        out_shape=jax.ShapeDtypeStruct((8, 16, 512), F32),
        in_specs=[any_spec] * 7 + [vmem_spec] * 3,
        out_specs=vmem_spec,
        scratch_shapes=scratch,
        compiler_params=pltpu.CompilerParams(
            collective_id=0, has_side_effects=True, vmem_limit_bytes=48 * 2**20
        ),
    )(right_side, inverse_density, *consts)


def solution(mesh):
    return jax.shard_map(
        local,
        mesh=mesh,
        in_specs=(P("gx", "gy", None), P("gx", "gy", None)),
        out_specs=P("gx", "gy", None),
        check_vma=False,
    )
```

time: 491 us -> 64.2 us (0.13)
  the two profiles are of different devices: /device:TPU:10 before, /device:TPU:1 now
where the time goes in v1:
time: 64.2 us; the launch traced here: 63.8 us
  Pallas kernels  53.1 us (83%)
  local copies, waits for them, and re-layouts  10.7 us (17%)
    pallas_call x1, Pallas kernels, local(): pl.pallas_call(kernel, out_shape=jax.ShapeDtypeStruct((8, 16, 512), F32),...  53.1 us
    unnamed x21, local copies, waits for them, and re-layouts  10.7 us

profile of v1, /device:TPU:1, one launch (start us, length us, event | category | flops | bytes accessed | tf_op | source)
XLA Modules:
  0.0 63.8 jit_solution(3980472535016927498)
XLA Ops:
  0.0 0.0 copy-start
  0.0 1.2 %copy-done = f32[32,64,64]{2,1,0:T(8,128)S(1)} copy-done((f32[32,64,64]{2,1,0:T(8,128)S(1)}, f32[32,64,64]{2,1,0:T(8,128)}, u32[]{:S(2)}) %copy-start) | copy-done | bytes 524312
  1.2 0.0 copy-start.1
  1.2 1.2 %copy-done.1 = f32[512,512]{1,0:T(8,128)S(1)} copy-done((f32[512,512]{1,0:T(8,128)S(1)}, f32[512,512]{1,0:T(8,128)}, u32[]{:S(2)}) %copy-start.1) | copy-done | bytes 1048600
  2.5 0.0 copy-start.2
  2.5 1.2 %copy-done.2 = f32[512,512]{1,0:T(8,128)S(1)} copy-done((f32[512,512]{1,0:T(8,128)S(1)}, f32[512,512]{1,0:T(8,128)}, u32[]{:S(2)}) %copy-start.2) | copy-done | bytes 1048600
  3.7 0.0 copy-start.3
  3.7 0.9 %copy-done.3 = f32[8,16,512]{2,1,0:T(8,128)S(1)} copy-done((f32[8,16,512]{2,1,0:T(8,128)S(1)}, f32[8,16,512]{2,1,0:T(8,128)}, u32[]{:S(2)}) %copy-start.3) | copy-done | bytes 262168
  4.6 0.0 copy-start.4
  4.6 0.9 %copy-done.4 = f32[8,16,512]{2,1,0:T(8,128)S(1)} copy-done((f32[8,16,512]{2,1,0:T(8,128)S(1)}, f32[8,16,512]{2,1,0:T(8,128)}, u32[]{:S(2)}) %copy-start.4) | copy-done | bytes 262168
  5.6 0.0 copy-start.5
  5.6 0.9 %copy-done.5 = f32[32,16,64]{2,1,0:T(8,128)S(1)} copy-done((f32[32,16,64]{2,1,0:T(8,128)S(1)}, f32[32,16,64]{2,1,0:T(8,128)}, u32[]{:S(2)}) %copy-start.5) | copy-done | bytes 131096
  6.5 0.0 copy-start.6
  6.5 0.9 %copy-done.6 = f32[128,256]{1,0:T(8,128)S(1)} copy-done((f32[128,256]{1,0:T(8,128)S(1)}, f32[128,256]{1,0:T(8,128)}, u32[]{:S(2)}) %copy-start.6) | copy-done | bytes 131096
  7.4 0.0 copy-start.7
  7.4 0.9 %copy-done.7 = f32[256,128]{1,0:T(8,128)S(1)} copy-done((f32[256,128]{1,0:T(8,128)S(1)}, f32[256,128]{1,0:T(8,128)}, u32[]{:S(2)}) %copy-start.7) | copy-done | bytes 131096
  8.3 0.0 copy-start.8
  8.3 0.9 %copy-done.8 = f32[64,512]{1,0:T(8,128)S(1)} copy-done((f32[64,512]{1,0:T(8,128)S(1)}, f32[64,512]{1,0:T(8,128)}, u32[]{:S(2)}) %copy-start.8) | copy-done | bytes 131096
  9.2 0.0 copy-start.9
  9.2 0.8 %copy-done.9 = f32[72,16]{1,0:T(8,128)S(1)} copy-done((f32[72,16]{1,0:T(8,128)S(1)}, f32[72,16]{1,0:T(8,128)}, u32[]{:S(2)}) %copy-start.9) | copy-done | bytes 4632
  10.0 53.1 %shard_map.100 = f32[8,16,512]{2,1,0:T(8,128)S(1)} custom-call(f32[8,16,512]{2,1,0:T(8,128)S(1)} %copy-done.3, f32[8,16,512]{2,1,0:T(8,128)S(1)} %copy-done.4, f32[512,512]{1,0:T(8,128)S(1)} %copy-done.2, f32[512,512]{1,0:T(8,128)S(1)} %copy-done.1, f32[32,64,64]{2,1,0:T(8,128)S(1)} %copy-done, f32[32,16,64]{2,1,0:T(8,128)S(1)} %copy-done.5, ...), custom_call_target="tpu_custom_call" | custom-call | tf_op jit(solution)/shard_map/pallas_call | solution.py:507
  63.1 0.7 %copy.12 = f32[8,16,512]{2,1,0:T(8,128)} copy(f32[8,16,512]{2,1,0:T(8,128)S(1)} %shard_map.100) | data formatting | bytes 524288
Async XLA Ops:
  0.0 1.2 %copy-start = (f32[32,64,64]{2,1,0:T(8,128)S(1)}, f32[32,64,64]{2,1,0:T(8,128)}, u32[]{:S(2)}) copy-start(f32[32,64,64]{2,1,0:T(8,128)} %constant.18.clone.turn_in) | copy-start | bytes 1572868
  1.2 1.2 %copy-start.1 = (f32[512,512]{1,0:T(8,128)S(1)}, f32[512,512]{1,0:T(8,128)}, u32[]{:S(2)}) copy-start(f32[512,512]{1,0:T(8,128)} %constant.17.clone.inv_in) | copy-start | bytes 3145732
  2.5 1.2 %copy-start.2 = (f32[512,512]{1,0:T(8,128)S(1)}, f32[512,512]{1,0:T(8,128)}, u32[]{:S(2)}) copy-start(f32[512,512]{1,0:T(8,128)} %constant.16.clone.fwd_in) | copy-start | bytes 3145732
  3.7 0.9 %copy-start.3 = (f32[8,16,512]{2,1,0:T(8,128)S(1)}, f32[8,16,512]{2,1,0:T(8,128)}, u32[]{:S(2)}) copy-start(f32[8,16,512]{2,1,0:T(8,128)} %r_in.1) | copy-start | bytes 786436
  4.6 0.9 %copy-start.4 = (f32[8,16,512]{2,1,0:T(8,128)S(1)}, f32[8,16,512]{2,1,0:T(8,128)}, u32[]{:S(2)}) copy-start(f32[8,16,512]{2,1,0:T(8,128)} %b_in.1) | copy-start | bytes 786436
  5.6 0.9 %copy-start.5 = (f32[32,16,64]{2,1,0:T(8,128)S(1)}, f32[32,16,64]{2,1,0:T(8,128)}, u32[]{:S(2)}) copy-start(f32[32,16,64]{2,1,0:T(8,128)} %constant.19.clone.wind_in) | copy-start | bytes 393220
  6.5 0.9 %copy-start.6 = (f32[128,256]{1,0:T(8,128)S(1)}, f32[128,256]{1,0:T(8,128)}, u32[]{:S(2)}) copy-start(f32[128,256]{1,0:T(8,128)} %constant.22.clone.grow) | copy-start | bytes 393220
  7.4 0.9 %copy-start.7 = (f32[256,128]{1,0:T(8,128)S(1)}, f32[256,128]{1,0:T(8,128)}, u32[]{:S(2)}) copy-start(f32[256,128]{1,0:T(8,128)} %constant.21.clone.pair) | copy-start | bytes 393220
  8.3 0.9 %copy-start.8 = (f32[64,512]{1,0:T(8,128)S(1)}, f32[64,512]{1,0:T(8,128)}, u32[]{:S(2)}) copy-start(f32[64,512]{1,0:T(8,128)} %constant.20.clone.table_in) | copy-start | bytes 393220
  9.2 0.8 %copy-start.9 = (f32[72,16]{1,0:T(8,128)S(1)}, f32[72,16]{1,0:T(8,128)}, u32[]{:S(2)}) copy-start(f32[72,16]{1,0:T(8,128)} %constant.23.clone.rows) | copy-start | bytes 13828

commit v2 on v1

--- a/solution.py
+++ b/solution.py
@@ -18,6 +18,7 @@
 C_OLD = RHO1 * RHO0
 C_NEW = 2.0 * RHO1 / DELTA
 GX, GY = 8, 32
+UNROLL = 2
 NEIGHBOURS = [(a, b) for a in (-1, 0, 1) for b in (-1, 0, 1) if (a, b) != (0, 0)]
 BRICKS = [(a, b) for a in range(GX) for b in (-1, 0, 1) if (a, b) != (0, 0)]
 LINE = [(0, b) for b in range(1, GY)]
@@ -34,10 +35,11 @@
 
 
 def constants():
-    cx, cy, cz = dct_matrix(8), dct_matrix(64), dct_matrix(64)
-    forward = np.einsum("ax,cz->xzac", cx, cz).reshape(512, 512)
+    cy, cz = dct_matrix(64), dct_matrix(64)
+    along = np.kron(np.eye(2), cz.T)
     turned = np.stack([np.roll(cy, 32 - 2 * g, axis=1) for g in range(GY)])
-    window = np.stack([t.T[24:40] for t in turned])
+    window = np.stack([np.pad(t.T[24:40], ((0, 0), (0, 64))) for t in turned])
+    turned = np.pad(turned, ((0, 0), (0, 0), (0, 64)))
     lam = [2 - 2 * np.cos(np.pi * np.arange(n) / n) for n in (8, 64, 64)]
     total = (lam[1][:, None, None] + lam[0][None, :, None] + lam[2][None, None, :]) * 4.0**-3
     total[0, 0, 0] = 1.0
@@ -47,22 +49,16 @@
     pair[np.arange(256), np.arange(256) // 2] = 0.125
     grow = np.zeros((128, 256))
     grow[np.arange(256) // 2, np.arange(256)] = 1.0
-    rows = np.zeros((72, 16))
-    for j in range(24):
-        if 2 <= j < 22:
-            rows[j, (j + 4) // 2] = 1.0
-    for j in range(16):
-        rows[24 + j, 2 + j // 2] = 1.0
-    for j in range(12):
-        rows[40 + j, 6 + j // 2] = 1.0
-    for j in range(8):
-        rows[56 + j, 2 * j] = 1.0
-        rows[56 + j, 2 * j + 1] = 1.0
-    for j in range(2):
-        rows[64 + j, 4 + 2 * j] = 1.0
-        rows[64 + j, 5 + 2 * j] = 1.0
-    out = (forward, forward.T, turned, window, table.reshape(64, 512), pair, grow, rows)
-    return tuple(np.ascontiguousarray(v, dtype=np.float32) for v in out)
+    cx = dct_matrix(8)
+    cross = np.zeros((2, 2, 4, 4, 128))
+    for i in range(4):
+        for j in range(4):
+            for k, c in enumerate((cx, cx.T)):
+                cross[k, 0, i, j] = np.repeat([c[2 * i, 2 * j], c[2 * i + 1, 2 * j + 1]], 64)
+                cross[k, 1, i, j] = np.repeat([c[2 * i, 2 * j + 1], c[2 * i + 1, 2 * j]], 64)
+    out = (along, along.T, turned, window, table.reshape(64, 512), cross.reshape(64, 128))
+    out = tuple(np.ascontiguousarray(v, dtype=np.float32) for v in out)
+    return out + (pair.astype(jnp.bfloat16), grow.astype(jnp.bfloat16))
 
 
 def device(offset):
@@ -85,6 +81,54 @@
 
 def down(value, axis, step=1):
     return pltpu.roll(value, step, axis)
+
+
+def parts(value):
+    high = value.astype(jnp.bfloat16)
+    return high, (value - high.astype(F32)).astype(jnp.bfloat16)
+
+
+def pick(value, matrix):
+    high, low = parts(value)
+    return jnp.dot(high, matrix, preferred_element_type=F32) + jnp.dot(
+        low, matrix, preferred_element_type=F32
+    )
+
+
+def halve(ref, base, value):
+    tiles = []
+    for t in range(value.shape[-1] // 128):
+        ref[base + t, 0 : value.shape[0], :] = value[:, 128 * t : 128 * t + 128]
+        count = value.shape[0] // 2
+        tiles.append(
+            ref[base + t, pl.ds(0, count, stride=2), :] + ref[base + t, pl.ds(1, count, stride=2), :]
+        )
+    return tiles
+
+
+def double(ref, base, value, low, count):
+    n = value.shape[0]
+    tiles = []
+    for t in range(value.shape[-1] // 128):
+        v = value[:, 128 * t : 128 * t + 128]
+        ref[base + t, pl.ds(4, n, stride=2), :] = v
+        ref[base + t, pl.ds(5, n, stride=2), :] = v
+        tiles.append(ref[base + t, low : low + count, :])
+    return jnp.concatenate(tiles, axis=1)
+
+
+def cross_x(value, cross, k):
+    v = [value[:, 128 * t : 128 * t + 128] for t in range(4)]
+    w = [pltpu.roll(t, 64, 1) for t in v]
+    out = []
+    for i in range(4):
+        acc = None
+        for j in range(4):
+            row = 32 * k + 4 * i + j
+            term = v[j] * cross[row : row + 1, :] + w[j] * cross[row + 16 : row + 17, :]
+            acc = term if acc is None else acc + term
+        out.append(acc)
+    return out
 
 
 def dot(a, b):
@@ -129,6 +173,30 @@
     return copies
 
 
+def brick_copies(src, dst, side, h, send, recv):
+    copies = []
+    for k, (a, b) in enumerate(NEIGHBOURS):
+        x = {0: pl.ds(0, 8), 1: pl.ds(8 - h, h), -1: pl.ds(0, h)}[a]
+        y = {0: pl.ds(0, 16), 1: pl.ds(16 - h, h), -1: pl.ds(0, h)}[b]
+        if b == 0:
+            to = side.at[pl.ds(0 if a > 0 else h, h), :, :]
+        else:
+            put_x = {0: pl.ds(3, 8), 1: pl.ds(3 - h, h), -1: pl.ds(11, h)}[a]
+            put_y = {1: pl.ds(4 - h, h), -1: pl.ds(20, h)}[b]
+            to = dst.at[put_x, put_y, :]
+        copies.append(
+            pltpu.make_async_remote_copy(
+                src.at[x, y, :],
+                to,
+                send.at[k],
+                recv.at[k],
+                device_id=device((a, b)),
+                device_id_type=MESH,
+            )
+        )
+    return copies
+
+
 def start(copies):
     for c in copies:
         c.start()
@@ -168,21 +236,20 @@
 
 
 def kernel(
-    r_in, b_in, fwd_in, inv_in, turn_in, wind_in, table_in, pair, grow, rows, out,
-    b0, r0, wx0, wy0, wz0, g0, d0, e0, q0, xp0, y0,
+    r_in, b_in, fwd_in, inv_in, turn_in, wind_in, table_in, cross_in, pair_in, grow_in, out,
+    bs, rs, xb, xr, b0, r0, wx0, wy0, wz0, g0, d0, e0, q0, xp0, y0, thin,
     b1, r1, xp1, b2, r2, xp2, e2, m2, b3, r3, m3,
-    fwd, inv, turn, wind, table,
+    fwd, inv, turn, wind, table, cross, pair, grow,
     local, halo_s, halo_r, many_s, many_r,
 ):
     gx, gy = lax.axis_index("gx"), lax.axis_index("gy")
     own = [
-        pltpu.make_async_copy(
-            src.at[:, pl.ds(4 * j, 4), :],
-            dst.at[pl.ds(3, 8), pl.ds(4 + 4 * j, 4), :],
-            local.at[k, j],
-        )
-        for k, (src, dst) in enumerate(((b_in, b0), (r_in, r0)))
-        for j in range(4)
+        pltpu.make_async_copy(b_in, bs, local.at[0, 0]),
+        pltpu.make_async_copy(r_in, rs, local.at[0, 1]),
+    ]
+    small = [
+        pltpu.make_async_copy(pair_in, pair, local.at[3, 2]),
+        pltpu.make_async_copy(grow_in, grow, local.at[3, 3]),
     ]
     fixed = [
         pltpu.make_async_copy(fwd_in, fwd, local.at[2, 0]),
@@ -190,44 +257,22 @@
         pltpu.make_async_copy(turn_in.at[gy], turn, local.at[2, 2]),
         pltpu.make_async_copy(wind_in.at[gy], wind, local.at[2, 3]),
         pltpu.make_async_copy(table_in, table, local.at[3, 0]),
+        pltpu.make_async_copy(cross_in, cross, local.at[3, 1]),
     ]
-    start(own + fixed)
+    start(own + small + fixed)
     barrier = pltpu.get_barrier_semaphore()
     for p in PEERS:
         pl.semaphore_signal(barrier, inc=1, device_id=device(p), device_id_type=MESH)
 
-    down0 = rows[56:64, :]
-    down2 = rows[64:72, :]
-
-    for c in own[:4]:
-        c.wait()
-    flat = []
-    for i in range(4):
-        s = b0[3 + 2 * i, 4:20, :] + b0[4 + 2 * i, 4:20, :]
-        flat.append(dot(down0, s))
-    flat = jnp.concatenate(flat, axis=0)
-    flat = jnp.concatenate([dot(flat[:, :256], pair[...]), dot(flat[:, 256:], pair[...])], axis=1)
-    for i in range(4):
-        b1[3 + i, 4:12, :] = flat[8 * i : 8 * i + 8]
-    half = rows[56:60, 0:8]
-    for i in range(2):
-        s = flat[16 * i : 16 * i + 8] + flat[16 * i + 8 : 16 * i + 16]
-        s = dot(dot(half, s), pair[...])
-        b2[2 * gx + i, 4:8, :] = s
-
-    for c in own[4:]:
-        c.wait()
     pl.semaphore_wait(barrier, len(PEERS))
-
-    b0_out = halo_copies(b0, (3, 4), (8, 16), (3, 3), halo_s.at[0], halo_r.at[0])
-    r0_out = halo_copies(r0, (3, 4), (8, 16), (2, 2), halo_s.at[1], halo_r.at[1])
+    b0_out = brick_copies(b_in, b0, xb, 3, halo_s.at[0], halo_r.at[0])
+    r0_out = brick_copies(r_in, r0, xr, 2, halo_s.at[1], halo_r.at[1])
     b1_out = halo_copies(b1, (3, 4), (4, 8), (3, 4), halo_s.at[2], halo_r.at[2])
     r1_out = halo_copies(r1, (3, 4), (4, 8), (2, 2), halo_s.at[3], halo_r.at[3])
     xp0_out = halo_copies(xp0, (3, 4), (8, 16), (2, 2), halo_s.at[4], halo_r.at[4])
     xp1_out = halo_copies(xp1, (3, 4), (4, 8), (3, 3), halo_s.at[5], halo_r.at[5])
     start(b0_out)
     start(r0_out)
-    start(b1_out)
 
     def bricks(ref, k):
         for a, b in BRICKS:
@@ -256,9 +301,49 @@
             ref, ref, many_s.at[k], many_r.at[k], device_id=device((0, 1)), device_id_type=MESH
         )
 
+    for c in small:
+        c.wait()
+    own[0].wait()
+
+    @pl.loop(0, 8, unroll=True)
+    def _(i):
+        b0[i + 3, 4:20, :] = bs[i]
+
+    def coarse0(planes, dst):
+        tiles = [halve(thin, 4 * i, planes[i]) for i in range(4)]
+        wide = [jnp.concatenate([tiles[i][t] for i in range(4)], axis=0) for t in range(4)]
+        low = pick(jnp.concatenate(wide[:2], axis=1), pair[...])
+        high = pick(jnp.concatenate(wide[2:], axis=1), pair[...])
+        for i in range(4):
+            dst[3 + i, 4:12, 0:128] = low[8 * i : 8 * i + 8]
+            dst[3 + i, 4:12, 128:256] = high[8 * i : 8 * i + 8]
+        return jnp.concatenate([low, high], axis=1)
+
+    def coarse1(planes, dst):
+        tiles = [halve(thin, 2 * i, planes[i]) for i in range(2)]
+        wide = [jnp.concatenate([tiles[i][t] for i in range(2)], axis=0) for t in range(2)]
+        low = pick(jnp.concatenate(wide, axis=1), pair[...])
+        for i in range(2):
+            dst[2 * gx + i, 4:8, :] = low[4 * i : 4 * i + 4]
+
+    flat = coarse0([bs[2 * i] + bs[2 * i + 1] for i in range(4)], b1)
+    coarse1([flat[16 * i : 16 * i + 8] + flat[16 * i + 8 : 16 * i + 16] for i in range(2)], b2)
+    start(b1_out)
     bricks(b2, 0)
+    own[1].wait()
+
+    @pl.loop(0, 8, unroll=True)
+    def _(i):
+        r0[i + 3, 4:20, :] = rs[i]
+
     arrive(b0_out)
     arrive(r0_out)
+    for i in range(3):
+        b0[i, 4:20, :] = xb[i]
+        b0[11 + i, 4:20, :] = xb[3 + i]
+    for i in range(2):
+        r0[1 + i, 4:20, :] = xr[i]
+        r0[11 + i, 4:20, :] = xr[2 + i]
 
     row = iota((24, 512), 0)
     lane = iota((24, 512), 1)
@@ -269,7 +354,7 @@
 
     wx0[0] = 2.0 * harm(b0[0], b0[1])
 
-    @pl.loop(1, 13)
+    @pl.loop(1, 13, unroll=UNROLL)
     def _(i):
         c = b0[i]
         wx = harm(c, b0[i + 1]) * jnp.where(i == cut0, 0.0, 2.0)
@@ -289,27 +374,20 @@
         fx = wx0[i] * (ref[i + 1] - c) - wx0[i - 1] * (c - ref[i - 1])
         return fx + (fy - down(fy, 0)) + (fz - down(fz, 1))
 
-    @pl.loop(2, 12)
+    @pl.loop(2, 12, unroll=UNROLL)
     def _(i):
         q = r0[i] + op0(d0, i)
         q0[i] = q
         e0[i] = C_OLD * d0[i] + C_NEW * (g0[i] * q)
 
-    @pl.loop(3, 11)
+    @pl.loop(3, 11, unroll=UNROLL)
     def _(i):
         q = q0[i] + op0(e0, i)
         q0[i] = q
         x = d0[i] + e0[i]
         xp0[i, 4:20, :] = x[4:20]
 
-    flat = []
-    for i in range(4):
-        s = q0[3 + 2 * i, 4:20, :] + q0[4 + 2 * i, 4:20, :]
-        flat.append(dot(down0, s))
-    flat = jnp.concatenate(flat, axis=0)
-    flat = jnp.concatenate([dot(flat[:, :256], pair[...]), dot(flat[:, 256:], pair[...])], axis=1)
-    for i in range(4):
-        r1[3 + i, 4:12, :] = flat[8 * i : 8 * i + 8]
+    coarse0([(q0[3 + 2 * i] + q0[4 + 2 * i])[4:20] for i in range(4)], r1)
     start(r1_out)
     start(xp0_out)
 
@@ -331,13 +409,18 @@
 
     def to_flat(value):
         value = jnp.where(iota((16, 16, 128), 1) < 8, value, 0.0)
-        parts = []
-        for t in range(4):
-            s = jnp.concatenate(
-                [value[4 * t] + value[4 * t + 1], value[4 * t + 2] + value[4 * t + 3]], axis=1
-            )
-            parts.append(dot(s, pair[...]))
-        return dot(down2, jnp.concatenate(parts, axis=1))[0:2]
+        wide = jnp.concatenate(
+            [
+                jnp.concatenate(
+                    [value[4 * t] + value[4 * t + 1], value[4 * t + 2] + value[4 * t + 3]], axis=1
+                )
+                for t in range(4)
+            ],
+            axis=0,
+        )
+        wide = pick(wide, pair[...])
+        tiles = [halve(thin, t, wide[16 * t : 16 * t + 16])[0][2:4] for t in range(4)]
+        return jnp.concatenate(tiles, axis=1)
 
     v = b2[...]
     b3[32:34, :] = to_flat(v)
@@ -361,10 +444,7 @@
     e = C_OLD * d[1:7] + C_NEW * (g1[1:7] * q)
     q = q[1:5] + planes_op(e, wx1[2:7], wy1[2:8], wz1[2:8], 1, 5)
     xp1[3:7, 4:12, :] = (d[2:6] + e[1:5])[:, 4:12, :]
-    for i in range(2):
-        s = (q[2 * i] + q[2 * i + 1])[4:12]
-        s = dot(dot(half, s), pair[...])
-        r2[2 * gx + i, 4:8, :] = s
+    coarse1([(q[2 * i] + q[2 * i + 1])[4:12] for i in range(2)], r2)
     bricks(r2, 1)
     start(xp1_out)
 
@@ -410,8 +490,14 @@
     q = f3 + flat_op(d, wx3, wy3, wz3)
     e = C_OLD * d + C_NEW * (g3 * q)
     q = q + flat_op(e, wx3, wy3, wz3)
-    t = dot(dot(turn[...], q), fwd[...]) * table[...]
-    t = dot(dot(wind[...], t), inv[...])
+    t = jnp.concatenate([q[:, 128 * t : 128 * t + 128] for t in range(4)], axis=0)
+    t = dot(t, fwd[...])
+    t = jnp.concatenate([t[64 * i : 64 * i + 64] for i in range(4)], axis=1)
+    t = jnp.concatenate(cross_x(t, cross, 0), axis=1)
+    t = dot(turn[:, 0:64], t) * table[...]
+    t = dot(wind[:, 0:64], t)
+    t = dot(jnp.concatenate(cross_x(t, cross, 1), axis=0), inv[...])
+    t = jnp.concatenate([t[16 * i : 16 * i + 16] for i in range(4)], axis=1)
     w = slice(24, 40)
     x = d[w] + e[w] + t
     w3 = (wx3[w], wy3[w], wz3[w])
@@ -420,22 +506,25 @@
     q = q + flat_op(d, *w3)
     x = x + d + (C_OLD * d + C_NEW * (g3[w] * q))
 
-    x = dot(rows[40:56, :], x)
-    wide = [dot(x[:, 128 * t : 128 * t + 128], grow[...]) for t in range(4)]
-    wide = jnp.stack([wide[i // 4][:, 128 * (i // 2 % 2) : 128 * (i // 2 % 2) + 128] for i in range(16)])
+    wide = pick(
+        jnp.concatenate([x[:, 128 * t : 128 * t + 128] for t in range(4)], axis=0), grow[...]
+    )
+    wide = [double(thin, 2 * t, wide[16 * t : 16 * t + 16], 16, 16) for t in range(4)]
+    wide = jnp.stack(
+        [wide[i // 4][:, 128 * (i // 2 % 2) : 128 * (i // 2 % 2) + 128] for i in range(16)]
+    )
     arrive(xp2_out)
     x = xp2[...] + wide
     q = f2 + ring_op(x, wx2, wy2, wz2)
     d = g2 * q * C_FIRST
     q = q + ring_op(d, wx2, wy2, wz2)
     x = x + d + (C_OLD * d + C_NEW * (g2 * q))
-    line = iota((16, 16, 128), 1)
-    x = jnp.where((line >= 2) & (line < 10), x, 0.0)
     e2[2:18] = x
     e2[0:2] = x[14:16]
     e2[18:20] = x[0:2]
 
-    wide = [dot(rows[24:40, :], dot(e2[2 * gx + i], grow[...])) for i in range(6)]
+    wide = pick(jnp.concatenate([e2[2 * gx + i] for i in range(6)], axis=0), grow[...])
+    wide = [double(thin, 2 * i, wide[16 * i : 16 * i + 16], 8, 16) for i in range(6)]
     wide = jnp.stack([wide[(i + 1) // 2] for i in range(10)])
     arrive(xp1_out)
     x = xp1[...] + wide
@@ -443,25 +532,25 @@
     d = g1 * q * C_FIRST
     q = q[1:7] + planes_op(d, wx1[1:8], wy1[1:9], wz1[1:9], 1, 7)
     x = x[2:8] + d[1:7] + (C_OLD * d[1:7] + C_NEW * (g1[1:7] * q))
-    line = iota((6, 16, 256), 1)
-    x = jnp.where((line >= 3) & (line < 13), x, 0.0)
-
+
+    low = pick(jnp.concatenate([x[i, :, :128] for i in range(6)], axis=0), grow[...])
+    high = pick(jnp.concatenate([x[i, :, 128:] for i in range(6)], axis=0), grow[...])
+    wide = jnp.concatenate([low, high], axis=1)
     for i in range(6):
-        s = dot(rows[0:24, :], x[i])
-        y0[i] = jnp.concatenate([dot(s[:, :128], grow[...]), dot(s[:, 128:], grow[...])], axis=1)
+        y0[i] = double(thin, 4 * i, wide[16 * i : 16 * i + 16], 8, 24)
     arrive(xp0_out)
 
-    @pl.loop(1, 13)
+    @pl.loop(1, 13, unroll=UNROLL)
     def _(i):
         e0[i] = xp0[i] + y0[(i + 3) // 2 - 2]
 
-    @pl.loop(2, 12)
+    @pl.loop(2, 12, unroll=UNROLL)
     def _(i):
         q = r0[i] + op0(e0, i)
         q0[i] = q
         d0[i] = g0[i] * q * C_FIRST
 
-    @pl.loop(3, 11)
+    @pl.loop(3, 11, unroll=UNROLL)
     def _(i):
         q = q0[i] + op0(d0, i)
         d = d0[i]
@@ -477,11 +566,14 @@
 
 def local(right_side, inverse_density):
     consts = constants()
-    any_spec = pl.BlockSpec(memory_space=pl.ANY)
+    far_spec = pl.BlockSpec(memory_space=pltpu.HBM)
     vmem_spec = pl.BlockSpec(memory_space=pltpu.VMEM)
     fine = pltpu.VMEM((14, 24, 512), F32)
-    scratch = [fine] * 10 + [
+    scratch = [pltpu.VMEM((8, 16, 512), F32)] * 2
+    scratch += [pltpu.VMEM((6, 16, 512), F32), pltpu.VMEM((4, 16, 512), F32)]
+    scratch += [fine] * 10 + [
         pltpu.VMEM((6, 24, 512), F32),
+        pltpu.VMEM((24, 40, 128), F32),
         pltpu.VMEM((10, 16, 256), F32),
         pltpu.VMEM((10, 16, 256), F32),
         pltpu.VMEM((10, 16, 256), F32),
@@ -493,11 +585,14 @@
         pltpu.VMEM((64, 512), F32),
         pltpu.VMEM((64, 512), F32),
         pltpu.VMEM((len(LINE), 8, 128), F32),
-        pltpu.VMEM((512, 512), F32),
-        pltpu.VMEM((512, 512), F32),
-        pltpu.VMEM((64, 64), F32),
-        pltpu.VMEM((16, 64), F32),
+        pltpu.VMEM((128, 128), F32),
+        pltpu.VMEM((128, 128), F32),
+        pltpu.VMEM((64, 128), F32),
+        pltpu.VMEM((16, 128), F32),
         pltpu.VMEM((64, 512), F32),
+        pltpu.VMEM((64, 128), F32),
+        pltpu.VMEM((256, 128), jnp.bfloat16),
+        pltpu.VMEM((128, 256), jnp.bfloat16),
         pltpu.SemaphoreType.DMA((4, 4)),
         pltpu.SemaphoreType.DMA((7, 12)),
         pltpu.SemaphoreType.DMA((7, 12)),
@@ -507,11 +602,11 @@
     return pl.pallas_call(
         kernel,
         out_shape=jax.ShapeDtypeStruct((8, 16, 512), F32),
-        in_specs=[any_spec] * 7 + [vmem_spec] * 3,
+        in_specs=[far_spec] * 10,
         out_specs=vmem_spec,
         scratch_shapes=scratch,
         compiler_params=pltpu.CompilerParams(
-            collective_id=0, has_side_effects=True, vmem_limit_bytes=48 * 2**20
+            collective_id=0, has_side_effects=True, vmem_limit_bytes=63 * 2**20
         ),
     )(right_side, inverse_density, *consts)
 

time: 64.2 us -> 47.2 us (0.74)
  local copies, waits for them, and re-layouts: 10.7 us -> 1.67 us
  Pallas kernels: 53.1 us -> 45.4 us
    unnamed x21 -> x1, local copies, waits for them, and re-layouts: 10.7 us -> 1.67 us
    pallas_call x1, Pallas kernels: 53.1 us -> 45.4 us  [local(): pl.pallas_call(kernel, out_shape=jax.ShapeDtypeStruct((8, 16, 512), F32),...]
where the time goes in v2:
time: 47.2 us; the launch traced here: 47.1 us
  Pallas kernels  45.4 us (96%)
  local copies, waits for them, and re-layouts  1.67 us (4%)
    pallas_call x1, Pallas kernels, local(): pl.pallas_call(kernel, out_shape=jax.ShapeDtypeStruct((8, 16, 512), F32),...  45.4 us
    unnamed x1, local copies, waits for them, and re-layouts  1.67 us

profile of v2, /device:TPU:1, one launch (start us, length us, event | category | flops | bytes accessed | tf_op | source)
XLA Modules:
  0.0 47.1 jit_solution(14160042805411018511)
XLA Ops:
  0.0 45.4 %shard_map.100 = f32[8,16,512]{2,1,0:T(8,128)} custom-call(f32[8,16,512]{2,1,0:T(8,128)} %r_in.1, f32[8,16,512]{2,1,0:T(8,128)} %b_in.1, f32[128,128]{1,0:T(8,128)} %constant.16.clone.fwd_in, f32[128,128]{1,0:T(8,128)} %constant.17.clone.inv_in, f32[32,64,128]{2,1,0:T(8,128)} %constant.18.clone.turn_in, f32[32,16,128]{2,1,0:T(8,128)} %constant.19.clone.wind_in, ...), custom_call_target="tpu_custom_call" | custom-call | tf_op jit(solution)/shard_map/pallas_call | solution.py:602
  45.4 1.7 %copy.12 = f32[8,16,512]{2,1,0:T(8,128)} copy(f32[8,16,512]{2,1,0:T(8,128)} %shard_map.100) | data formatting | bytes 524288

commit v3 on v2

--- a/solution.py
+++ b/solution.py
@@ -18,13 +18,16 @@
 C_OLD = RHO1 * RHO0
 C_NEW = 2.0 * RHO1 / DELTA
 GX, GY = 8, 32
-UNROLL = 2
+UNROLL = True
 NEIGHBOURS = [(a, b) for a in (-1, 0, 1) for b in (-1, 0, 1) if (a, b) != (0, 0)]
-BRICKS = [(a, b) for a in range(GX) for b in (-1, 0, 1) if (a, b) != (0, 0)]
+COLUMN = [(a, 0) for a in range(1, GX)]
 LINE = [(0, b) for b in range(1, GY)]
-PEERS = list(
-    dict.fromkeys((a % GX, b % GY) for a, b in NEIGHBOURS + BRICKS + LINE)
-)
+ROUNDS = [
+    [(1, 0), (-1, 0), (0, 1), (0, -1)],
+    [(2, 0), (-2, 0), (0, 2), (0, -2)],
+    [(0, 4), (0, -4)],
+    [(0, 8), (0, -8)],
+]
 
 
 def dct_matrix(count):
@@ -106,13 +109,13 @@
     return tiles
 
 
-def double(ref, base, value, low, count):
+def double(ref, base, value, at, low, count):
     n = value.shape[0]
     tiles = []
     for t in range(value.shape[-1] // 128):
         v = value[:, 128 * t : 128 * t + 128]
-        ref[base + t, pl.ds(4, n, stride=2), :] = v
-        ref[base + t, pl.ds(5, n, stride=2), :] = v
+        ref[base + t, pl.ds(at, n, stride=2), :] = v
+        ref[base + t, pl.ds(at + 1, n, stride=2), :] = v
         tiles.append(ref[base + t, low : low + count, :])
     return jnp.concatenate(tiles, axis=1)
 
@@ -139,11 +142,11 @@
     return lax.broadcasted_iota(jnp.int32, shape, axis)
 
 
-def halo_copies(ref, at, size, halo, send, recv):
+def halo_copies(ref, at, size, halo, corner, send, recv):
     copies = []
     for a, b in NEIGHBOURS:
         take, put = [], []
-        for side, s0, n, h in zip((a, b), at, size, halo):
+        for side, s0, n, h in zip((a, b), at, size, corner if a != 0 and b != 0 else halo):
             if side == 0:
                 take.append((s0, n))
                 put.append(s0)
@@ -154,10 +157,8 @@
                 take.append((s0, h))
                 put.append(s0 + n)
         (x_from, x_count), (y_from, y_count) = take
-        if b == 0:
-            ends = [y_from] + list(range(y_from + 4, y_from + y_count, 8)) + [y_from + y_count]
-        else:
-            ends = [y_from, y_from + y_count]
+        y_end = y_from + y_count
+        ends = [y_from] + list(range(y_from // 8 * 8 + 8, y_end, 8)) + [y_end]
         for low, high in zip(ends[:-1], ends[1:]):
             k = len(copies)
             copies.append(
@@ -173,9 +174,10 @@
     return copies
 
 
-def brick_copies(src, dst, side, h, send, recv):
+def brick_copies(src, dst, side, halo, send, recv):
     copies = []
     for k, (a, b) in enumerate(NEIGHBOURS):
+        h = halo - 1 if a != 0 and b != 0 else halo
         x = {0: pl.ds(0, 8), 1: pl.ds(8 - h, h), -1: pl.ds(0, h)}[a]
         y = {0: pl.ds(0, 16), 1: pl.ds(16 - h, h), -1: pl.ds(0, h)}[b]
         if b == 0:
@@ -237,10 +239,10 @@
 
 def kernel(
     r_in, b_in, fwd_in, inv_in, turn_in, wind_in, table_in, cross_in, pair_in, grow_in, out,
-    bs, rs, xb, xr, b0, r0, wx0, wy0, wz0, g0, d0, e0, q0, xp0, y0, thin,
-    b1, r1, xp1, b2, r2, xp2, e2, m2, b3, r3, m3,
+    ov, bs, rs, xb, xr, b0, r0, wx0, wy0, wz0, g0, d0, e0, q0, xp0, y0, thin,
+    b1, r1, xp1, b2, r2, xp2, rn2, e2, m2, b3, r3, m3,
     fwd, inv, turn, wind, table, cross, pair, grow,
-    local, halo_s, halo_r, many_s, many_r,
+    local, halo_s, halo_r, many_s, many_r, near, done,
 ):
     gx, gy = lax.axis_index("gx"), lax.axis_index("gy")
     own = [
@@ -261,27 +263,36 @@
     ]
     start(own + small + fixed)
     barrier = pltpu.get_barrier_semaphore()
-    for p in PEERS:
+    for p in NEIGHBOURS:
         pl.semaphore_signal(barrier, inc=1, device_id=device(p), device_id_type=MESH)
 
-    pl.semaphore_wait(barrier, len(PEERS))
+    pl.semaphore_wait(barrier, len(NEIGHBOURS))
+
+    def tell(k):
+        for p in ROUNDS[k]:
+            pl.semaphore_signal(near.at[k], inc=1, device_id=device(p), device_id_type=MESH)
+
+    def heard(k):
+        pl.semaphore_wait(near.at[k], len(ROUNDS[k]))
+
     b0_out = brick_copies(b_in, b0, xb, 3, halo_s.at[0], halo_r.at[0])
     r0_out = brick_copies(r_in, r0, xr, 2, halo_s.at[1], halo_r.at[1])
-    b1_out = halo_copies(b1, (3, 4), (4, 8), (3, 4), halo_s.at[2], halo_r.at[2])
-    r1_out = halo_copies(r1, (3, 4), (4, 8), (2, 2), halo_s.at[3], halo_r.at[3])
-    xp0_out = halo_copies(xp0, (3, 4), (8, 16), (2, 2), halo_s.at[4], halo_r.at[4])
-    xp1_out = halo_copies(xp1, (3, 4), (4, 8), (3, 3), halo_s.at[5], halo_r.at[5])
+    b1_out = halo_copies(b1, (3, 8), (4, 8), (3, 8), (3, 8), halo_s.at[2], halo_r.at[2])
+    r1_out = halo_copies(r1, (3, 8), (4, 8), (2, 6), (2, 5), halo_s.at[3], halo_r.at[3])
+    xp0_out = halo_copies(xp0, (3, 4), (8, 16), (2, 2), (1, 1), halo_s.at[4], halo_r.at[4])
+    xp1_out = halo_copies(xp1, (3, 8), (4, 8), (3, 3), (3, 3), halo_s.at[5], halo_r.at[5])
     start(b0_out)
     start(r0_out)
-
-    def bricks(ref, k):
-        for a, b in BRICKS:
+    tell(0)
+
+    def column(ref, k):
+        for a, _ in COLUMN:
             pltpu.make_async_remote_copy(
-                ref.at[pl.ds(2 * gx, 2), pl.ds(4, 4), :],
-                ref.at[pl.ds(2 * gx, 2), pl.ds(4 - 4 * b, 4), :],
+                ref.at[pl.ds(2 * gx, 2)],
+                ref.at[pl.ds(2 * gx, 2)],
                 many_s.at[k],
                 many_r.at[k],
-                device_id=device((a, b)),
+                device_id=device((a, 0)),
                 device_id_type=MESH,
             ).start()
 
@@ -315,8 +326,8 @@
         low = pick(jnp.concatenate(wide[:2], axis=1), pair[...])
         high = pick(jnp.concatenate(wide[2:], axis=1), pair[...])
         for i in range(4):
-            dst[3 + i, 4:12, 0:128] = low[8 * i : 8 * i + 8]
-            dst[3 + i, 4:12, 128:256] = high[8 * i : 8 * i + 8]
+            dst[3 + i, 8:16, 0:128] = low[8 * i : 8 * i + 8]
+            dst[3 + i, 8:16, 128:256] = high[8 * i : 8 * i + 8]
         return jnp.concatenate([low, high], axis=1)
 
     def coarse1(planes, dst):
@@ -324,12 +335,10 @@
         wide = [jnp.concatenate([tiles[i][t] for i in range(2)], axis=0) for t in range(2)]
         low = pick(jnp.concatenate(wide, axis=1), pair[...])
         for i in range(2):
-            dst[2 * gx + i, 4:8, :] = low[4 * i : 4 * i + 4]
-
-    flat = coarse0([bs[2 * i] + bs[2 * i + 1] for i in range(4)], b1)
-    coarse1([flat[16 * i : 16 * i + 8] + flat[16 * i + 8 : 16 * i + 16] for i in range(2)], b2)
+            dst[2 * gx + i] = low[16 * i : 16 * i + 16]
+
+    coarse0([bs[2 * i] + bs[2 * i + 1] for i in range(4)], b1)
     start(b1_out)
-    bricks(b2, 0)
     own[1].wait()
 
     @pl.loop(0, 8, unroll=True)
@@ -338,6 +347,8 @@
 
     arrive(b0_out)
     arrive(r0_out)
+    heard(0)
+    tell(1)
     for i in range(3):
         b0[i, 4:20, :] = xb[i]
         b0[11 + i, 4:20, :] = xb[3 + i]
@@ -389,14 +400,22 @@
 
     coarse0([(q0[3 + 2 * i] + q0[4 + 2 * i])[4:20] for i in range(4)], r1)
     start(r1_out)
-    start(xp0_out)
+    heard(1)
+    tell(2)
 
     arrive(b1_out)
     v = b1[...]
-    shape = (10, 16, 256)
-    edge = jnp.where(gy == GY - 1, 11, jnp.where(gy == 0, 3, -1))
+    blank = jnp.zeros((8, 256), F32)
+
+    def tall(value):
+        return jnp.concatenate([value, blank], axis=0)
+
+    coarse1([tall(v[3 + 2 * i] + v[4 + 2 * i]) for i in range(2)], b2)
+    column(b2, 0)
+    shape = (10, 24, 256)
+    edge = jnp.where(gy == GY - 1, 15, jnp.where(gy == 0, 7, -1))
     cut = jnp.where(gx == GX - 1, 6, jnp.where(gx == 0, 2, -1))
-    keep_x = jnp.where(iota((9, 16, 256), 0) == cut, 0.0, 0.5)
+    keep_x = jnp.where(iota((9, 24, 256), 0) == cut, 0.0, 0.5)
     wx1 = harm(v[:-1], v[1:]) * keep_x
     wy1 = harm(v, up(v, 1)) * jnp.where(iota(shape, 1) == edge, 0.0, 0.5)
     wz1 = harm(v, up(v, 2)) * jnp.where(iota(shape, 2) == 255, 0.0, 0.5)
@@ -404,6 +423,20 @@
     g1 = recip(
         (wx1[1:] + wx1[:-1]) + (wy1[c] + down(wy1[c], 1)) + (wz1[c] + down(wz1[c], 2))
     )
+
+    arrive(r1_out)
+    heard(2)
+    tell(3)
+    f1 = r1[...]
+    d = g1 * f1[1:9] * C_FIRST
+    q = f1[2:8] + planes_op(d, wx1[1:8], wy1[1:9], wz1[1:9], 1, 7)
+    e = C_OLD * d[1:7] + C_NEW * (g1[1:7] * q)
+    q = q[1:5] + planes_op(e, wx1[2:7], wy1[2:8], wz1[2:8], 1, 5)
+    xp1[3:7, 8:16, :] = (d[2:6] + e[1:5])[:, 8:16, :]
+    line = iota((24, 256), 0)
+    inside = (line >= 4) & (line < 20)
+    coarse1([tall(jnp.where(inside, q[2 * i] + q[2 * i + 1], 0.0)) for i in range(2)], r2)
+    column(r2, 1)
 
     all_of(m2, 0).wait_recv()
 
@@ -424,6 +457,7 @@
 
     v = b2[...]
     b3[32:34, :] = to_flat(v)
+    heard(3)
     lines(b3, 2)
     shape = (16, 16, 128)
     edge = jnp.where(gy == GY - 1, 7, jnp.where(gy == 0, 3, -1))
@@ -437,16 +471,32 @@
         + (wz2 + down(wz2, 2))
     )
 
-    arrive(r1_out)
-    f1 = r1[...]
-    d = g1 * f1[1:9] * C_FIRST
-    q = f1[2:8] + planes_op(d, wx1[1:8], wy1[1:9], wz1[1:9], 1, 7)
-    e = C_OLD * d[1:7] + C_NEW * (g1[1:7] * q)
-    q = q[1:5] + planes_op(e, wx1[2:7], wy1[2:8], wz1[2:8], 1, 5)
-    xp1[3:7, 4:12, :] = (d[2:6] + e[1:5])[:, 4:12, :]
-    coarse1([(q[2 * i] + q[2 * i + 1])[4:12] for i in range(2)], r2)
-    bricks(r2, 1)
+    all_of(m2, 1).wait_recv()
+    f2 = r2[...]
+    d = g2 * f2 * C_FIRST
+    q = f2 + ring_op(d, wx2, wy2, wz2)
+    e = C_OLD * d + C_NEW * (g2 * q)
+    q = q + ring_op(e, wx2, wy2, wz2)
+    xp2[:, 4:8, :] = (d + e)[:, 4:8, :]
+    rn2[:, 4:8, :] = f2[:, 4:8, :]
+    q = jnp.where(iota((16, 16, 128), 1) >= 4, q, 0.0)
+    r3[32:34, :] = to_flat(q)
+    lines(r3, 3)
+    xp2_out = [
+        pltpu.make_async_remote_copy(
+            ref.at[:, pl.ds(4, 4), :],
+            ref.at[:, pl.ds(4 - 4 * b, 4), :],
+            halo_s.at[6, 2 * j + k],
+            halo_r.at[6, 2 * j + k],
+            device_id=device((0, b)),
+            device_id_type=MESH,
+        )
+        for j, ref in enumerate((xp2, rn2))
+        for k, b in enumerate((-1, 1))
+    ]
+    start(xp2_out)
     start(xp1_out)
+    start(xp0_out)
 
     all_of(m3, 2).wait_recv()
     v = b3[...]
@@ -459,28 +509,10 @@
     wz3 = harm(v, up(v, 1)) * jnp.where(lax.rem(lane, 64) == 63, 0.0, scale)
     g3 = recip((wx3 + down(wx3, 1, 64)) + (wy3 + down(wy3, 0)) + (wz3 + down(wz3, 1)))
 
-    all_of(m2, 1).wait_recv()
-    f2 = r2[...]
-    d = g2 * f2 * C_FIRST
-    q = f2 + ring_op(d, wx2, wy2, wz2)
-    e = C_OLD * d + C_NEW * (g2 * q)
-    q = q + ring_op(e, wx2, wy2, wz2)
-    xp2[:, 4:8, :] = (d + e)[:, 4:8, :]
-    q = jnp.where(iota((16, 16, 128), 1) >= 4, q, 0.0)
-    r3[32:34, :] = to_flat(q)
-    lines(r3, 3)
-    xp2_out = [
-        pltpu.make_async_remote_copy(
-            xp2.at[:, pl.ds(4, 4), :],
-            xp2.at[:, pl.ds(4 - 4 * b, 4), :],
-            halo_s.at[6, k],
-            halo_r.at[6, k],
-            device_id=device((0, b)),
-            device_id_type=MESH,
-        )
-        for k, b in enumerate((-1, 1))
-    ]
-    start(xp2_out)
+    sent(b0_out + r0_out + b1_out + r1_out)
+    all_of(m2, 0).wait_send()
+    all_of(m2, 1).wait_send()
+    all_of(m3, 2).wait_send()
 
     for c in fixed:
         c.wait()
@@ -509,13 +541,13 @@
     wide = pick(
         jnp.concatenate([x[:, 128 * t : 128 * t + 128] for t in range(4)], axis=0), grow[...]
     )
-    wide = [double(thin, 2 * t, wide[16 * t : 16 * t + 16], 16, 16) for t in range(4)]
+    wide = [double(thin, 2 * t, wide[16 * t : 16 * t + 16], 4, 16, 16) for t in range(4)]
     wide = jnp.stack(
         [wide[i // 4][:, 128 * (i // 2 % 2) : 128 * (i // 2 % 2) + 128] for i in range(16)]
     )
     arrive(xp2_out)
     x = xp2[...] + wide
-    q = f2 + ring_op(x, wx2, wy2, wz2)
+    q = rn2[...] + ring_op(x, wx2, wy2, wz2)
     d = g2 * q * C_FIRST
     q = q + ring_op(d, wx2, wy2, wz2)
     x = x + d + (C_OLD * d + C_NEW * (g2 * q))
@@ -524,7 +556,7 @@
     e2[18:20] = x[0:2]
 
     wide = pick(jnp.concatenate([e2[2 * gx + i] for i in range(6)], axis=0), grow[...])
-    wide = [double(thin, 2 * i, wide[16 * i : 16 * i + 16], 8, 16) for i in range(6)]
+    wide = [double(thin, 2 * i, wide[16 * i : 16 * i + 16], 0, 0, 24) for i in range(6)]
     wide = jnp.stack([wide[(i + 1) // 2] for i in range(10)])
     arrive(xp1_out)
     x = xp1[...] + wide
@@ -537,8 +569,10 @@
     high = pick(jnp.concatenate([x[i, :, 128:] for i in range(6)], axis=0), grow[...])
     wide = jnp.concatenate([low, high], axis=1)
     for i in range(6):
-        y0[i] = double(thin, 4 * i, wide[16 * i : 16 * i + 16], 8, 24)
+        y0[i] = double(thin, 4 * i, wide[24 * i : 24 * i + 24], 4, 16, 24)
     arrive(xp0_out)
+    sent(xp0_out + xp1_out + xp2_out)
+    all_of(m3, 3).wait_send()
 
     @pl.loop(1, 13, unroll=UNROLL)
     def _(i):
@@ -555,33 +589,31 @@
         q = q0[i] + op0(d0, i)
         d = d0[i]
         x = e0[i] + d + (C_OLD * d + C_NEW * (g0[i] * q))
-        out[i - 3] = x[4:20]
-
-    sent(b0_out + r0_out + b1_out + r1_out + xp0_out + xp1_out + xp2_out)
-    all_of(m2, 0).wait_send()
-    all_of(m2, 1).wait_send()
-    all_of(m3, 2).wait_send()
-    all_of(m3, 3).wait_send()
+        ov[i - 3] = x[4:20]
+        pltpu.make_async_copy(ov.at[i - 3], out.at[i - 3], done.at[i - 3]).start()
+
+    for i in range(8):
+        pltpu.make_async_copy(ov.at[i], out.at[i], done.at[i]).wait()
 
 
 def local(right_side, inverse_density):
     consts = constants()
     far_spec = pl.BlockSpec(memory_space=pltpu.HBM)
-    vmem_spec = pl.BlockSpec(memory_space=pltpu.VMEM)
     fine = pltpu.VMEM((14, 24, 512), F32)
-    scratch = [pltpu.VMEM((8, 16, 512), F32)] * 2
+    scratch = [pltpu.VMEM((8, 16, 512), F32)] * 3
     scratch += [pltpu.VMEM((6, 16, 512), F32), pltpu.VMEM((4, 16, 512), F32)]
     scratch += [fine] * 10 + [
         pltpu.VMEM((6, 24, 512), F32),
-        pltpu.VMEM((24, 40, 128), F32),
-        pltpu.VMEM((10, 16, 256), F32),
-        pltpu.VMEM((10, 16, 256), F32),
-        pltpu.VMEM((10, 16, 256), F32),
+        pltpu.VMEM((24, 56, 128), F32),
+        pltpu.VMEM((10, 24, 256), F32),
+        pltpu.VMEM((10, 24, 256), F32),
+        pltpu.VMEM((10, 24, 256), F32),
+        pltpu.VMEM((16, 16, 128), F32),
         pltpu.VMEM((16, 16, 128), F32),
         pltpu.VMEM((16, 16, 128), F32),
         pltpu.VMEM((16, 16, 128), F32),
         pltpu.VMEM((20, 16, 128), F32),
-        pltpu.VMEM((len(BRICKS), 8, 128), F32),
+        pltpu.VMEM((2 * len(COLUMN), 16, 128), F32),
         pltpu.VMEM((64, 512), F32),
         pltpu.VMEM((64, 512), F32),
         pltpu.VMEM((len(LINE), 8, 128), F32),
@@ -598,12 +630,14 @@
         pltpu.SemaphoreType.DMA((7, 12)),
         pltpu.SemaphoreType.DMA((4,)),
         pltpu.SemaphoreType.DMA((4,)),
+        pltpu.SemaphoreType.REGULAR((4,)),
+        pltpu.SemaphoreType.DMA((8,)),
     ]
     return pl.pallas_call(
         kernel,
         out_shape=jax.ShapeDtypeStruct((8, 16, 512), F32),
         in_specs=[far_spec] * 10,
-        out_specs=vmem_spec,
+        out_specs=far_spec,
         scratch_shapes=scratch,
         compiler_params=pltpu.CompilerParams(
             collective_id=0, has_side_effects=True, vmem_limit_bytes=63 * 2**20

time: 47.2 us -> 43.3 us (0.917)
  Pallas kernels: 45.4 us -> 41.6 us
    pallas_call x1, Pallas kernels: 45.4 us -> 41.6 us  [local(): pl.pallas_call(kernel, out_shape=jax.ShapeDtypeStruct((8, 16, 512), F32),...]
where the time goes in v3:
time: 43.3 us; the launch traced here: 43.2 us
  Pallas kernels  41.6 us (96%)
  local copies, waits for them, and re-layouts  1.67 us (4%)
    pallas_call x1, Pallas kernels, local(): pl.pallas_call(kernel, out_shape=jax.ShapeDtypeStruct((8, 16, 512), F32),...  41.6 us
    unnamed x1, local copies, waits for them, and re-layouts  1.67 us

profile of v3, /device:TPU:1, one launch (start us, length us, event | category | flops | bytes accessed | tf_op | source)
XLA Modules:
  0.0 43.2 jit_solution(16763354823490017038)
XLA Ops:
  0.0 41.6 %shard_map.100 = f32[8,16,512]{2,1,0:T(8,128)} custom-call(f32[8,16,512]{2,1,0:T(8,128)} %r_in.1, f32[8,16,512]{2,1,0:T(8,128)} %b_in.1, f32[128,128]{1,0:T(8,128)} %constant.16.clone.fwd_in, f32[128,128]{1,0:T(8,128)} %constant.17.clone.inv_in, f32[32,64,128]{2,1,0:T(8,128)} %constant.18.clone.turn_in, f32[32,16,128]{2,1,0:T(8,128)} %constant.19.clone.wind_in, ...), custom_call_target="tpu_custom_call" | custom-call | tf_op jit(solution)/shard_map/pallas_call | solution.py:636
  41.6 1.7 %copy.12 = f32[8,16,512]{2,1,0:T(8,128)} copy(f32[8,16,512]{2,1,0:T(8,128)} %shard_map.100) | data formatting | bytes 524288

commit v4 on v3

--- a/solution.py
+++ b/solution.py
@@ -19,9 +19,19 @@
 C_NEW = 2.0 * RHO1 / DELTA
 GX, GY = 8, 32
 UNROLL = True
-NEIGHBOURS = [(a, b) for a in (-1, 0, 1) for b in (-1, 0, 1) if (a, b) != (0, 0)]
-COLUMN = [(a, 0) for a in range(1, GX)]
-LINE = [(0, b) for b in range(1, GY)]
+NEIGHBOURS = [(1, 1), (1, -1), (-1, 1), (-1, -1), (0, 1), (0, -1), (1, 0), (-1, 0)]
+COLUMN = [(a, 0) for a in (4, 5, 3, 6, 2, 7, 1)]
+
+
+def hops(b):
+    z = b % 8
+    x = b // 8
+    near = min(z, 8 - z) + min(x, 4 - x)
+    x = (x + 1) % 4
+    return near + min(z, 8 - z) + min(x, 4 - x) if z else 2 * near
+
+
+LINE = sorted([(0, b) for b in range(1, GY)], key=lambda p: -hops(p[1]))
 ROUNDS = [
     [(1, 0), (-1, 0), (0, 1), (0, -1)],
     [(2, 0), (-2, 0), (0, 2), (0, -2)],
@@ -261,7 +271,6 @@
         pltpu.make_async_copy(table_in, table, local.at[3, 0]),
         pltpu.make_async_copy(cross_in, cross, local.at[3, 1]),
     ]
-    start(own + small + fixed)
     barrier = pltpu.get_barrier_semaphore()
     for p in NEIGHBOURS:
         pl.semaphore_signal(barrier, inc=1, device_id=device(p), device_id_type=MESH)
@@ -281,9 +290,9 @@
     r1_out = halo_copies(r1, (3, 8), (4, 8), (2, 6), (2, 5), halo_s.at[3], halo_r.at[3])
     xp0_out = halo_copies(xp0, (3, 4), (8, 16), (2, 2), (1, 1), halo_s.at[4], halo_r.at[4])
     xp1_out = halo_copies(xp1, (3, 8), (4, 8), (3, 3), (3, 3), halo_s.at[5], halo_r.at[5])
-    start(b0_out)
-    start(r0_out)
+    start(b0_out[:4] + r0_out[:4] + b0_out[4:6] + r0_out[4:6] + b0_out[6:] + r0_out[6:])
     tell(0)
+    start(own + small + fixed)
 
     def column(ref, k):
         for a, _ in COLUMN:

time: 43.3 us -> 42.7 us (0.986)
  Pallas kernels: 41.6 us -> 40.9 us
    pallas_call x1, Pallas kernels: 41.6 us -> 40.9 us  [local(): pl.pallas_call(kernel, out_shape=jax.ShapeDtypeStruct((8, 16, 512), F32),...]
where the time goes in v4:
time: 42.7 us; the launch traced here: 42.6 us
  Pallas kernels  40.9 us (96%)
  local copies, waits for them, and re-layouts  1.67 us (4%)
    pallas_call x1, Pallas kernels, local(): pl.pallas_call(kernel, out_shape=jax.ShapeDtypeStruct((8, 16, 512), F32),...  40.9 us
    unnamed x1, local copies, waits for them, and re-layouts  1.67 us

profile of v4, /device:TPU:1, one launch (start us, length us, event | category | flops | bytes accessed | tf_op | source)
XLA Modules:
  0.0 42.6 jit_solution(3773257527692006681)
XLA Ops:
  0.0 40.9 %shard_map.100 = f32[8,16,512]{2,1,0:T(8,128)} custom-call(f32[8,16,512]{2,1,0:T(8,128)} %r_in.1, f32[8,16,512]{2,1,0:T(8,128)} %b_in.1, f32[128,128]{1,0:T(8,128)} %constant.16.clone.fwd_in, f32[128,128]{1,0:T(8,128)} %constant.17.clone.inv_in, f32[32,64,128]{2,1,0:T(8,128)} %constant.18.clone.turn_in, f32[32,16,128]{2,1,0:T(8,128)} %constant.19.clone.wind_in, ...), custom_call_target="tpu_custom_call" | custom-call | tf_op jit(solution)/shard_map/pallas_call | solution.py:645
  40.9 1.7 %copy.12 = f32[8,16,512]{2,1,0:T(8,128)} copy(f32[8,16,512]{2,1,0:T(8,128)} %shard_map.100) | data formatting | bytes 524288

commit v5 on v4

--- a/solution.py
+++ b/solution.py
@@ -290,7 +290,7 @@
     r1_out = halo_copies(r1, (3, 8), (4, 8), (2, 6), (2, 5), halo_s.at[3], halo_r.at[3])
     xp0_out = halo_copies(xp0, (3, 4), (8, 16), (2, 2), (1, 1), halo_s.at[4], halo_r.at[4])
     xp1_out = halo_copies(xp1, (3, 8), (4, 8), (3, 3), (3, 3), halo_s.at[5], halo_r.at[5])
-    start(b0_out[:4] + r0_out[:4] + b0_out[4:6] + r0_out[4:6] + b0_out[6:] + r0_out[6:])
+    start(b0_out + r0_out)
     tell(0)
     start(own + small + fixed)
 
@@ -355,15 +355,9 @@
         r0[i + 3, 4:20, :] = rs[i]
 
     arrive(b0_out)
-    arrive(r0_out)
-    heard(0)
-    tell(1)
     for i in range(3):
         b0[i, 4:20, :] = xb[i]
         b0[11 + i, 4:20, :] = xb[3 + i]
-    for i in range(2):
-        r0[1 + i, 4:20, :] = xr[i]
-        r0[11 + i, 4:20, :] = xr[2 + i]
 
     row = iota((24, 512), 0)
     lane = iota((24, 512), 1)
@@ -385,7 +379,17 @@
         wz0[i] = wz
         g = recip((wx + wx0[i - 1]) + (wy + down(wy, 0)) + (wz + down(wz, 1)))
         g0[i] = g
-        d0[i] = g * r0[i] * C_FIRST
+
+    arrive(r0_out)
+    heard(0)
+    tell(1)
+    for i in range(2):
+        r0[1 + i, 4:20, :] = xr[i]
+        r0[11 + i, 4:20, :] = xr[2 + i]
+
+    @pl.loop(1, 13, unroll=UNROLL)
+    def _(i):
+        d0[i] = g0[i] * r0[i] * C_FIRST
 
     def op0(ref, i):
         c = ref[i]
@@ -580,8 +584,6 @@
     for i in range(6):
         y0[i] = double(thin, 4 * i, wide[24 * i : 24 * i + 24], 4, 16, 24)
     arrive(xp0_out)
-    sent(xp0_out + xp1_out + xp2_out)
-    all_of(m3, 3).wait_send()
 
     @pl.loop(1, 13, unroll=UNROLL)
     def _(i):
@@ -601,6 +603,8 @@
         ov[i - 3] = x[4:20]
         pltpu.make_async_copy(ov.at[i - 3], out.at[i - 3], done.at[i - 3]).start()
 
+    sent(xp0_out + xp1_out + xp2_out)
+    all_of(m3, 3).wait_send()
     for i in range(8):
         pltpu.make_async_copy(ov.at[i], out.at[i], done.at[i]).wait()
 

time: 42.7 us -> 42.8 us (level)
  no operation moved by 1% of the time
where the time goes in v5:
time: 42.8 us; the launch traced here: 42.7 us
  Pallas kernels  41 us (96%)
  local copies, waits for them, and re-layouts  1.67 us (4%)
    pallas_call x1, Pallas kernels, local(): pl.pallas_call(kernel, out_shape=jax.ShapeDtypeStruct((8, 16, 512), F32),...  41 us
    unnamed x1, local copies, waits for them, and re-layouts  1.67 us

profile of v5, /device:TPU:1, one launch (start us, length us, event | category | flops | bytes accessed | tf_op | source)
XLA Modules:
  0.0 42.7 jit_solution(11841411343828512758)
XLA Ops:
  0.0 41.0 %shard_map.100 = f32[8,16,512]{2,1,0:T(8,128)} custom-call(f32[8,16,512]{2,1,0:T(8,128)} %r_in.1, f32[8,16,512]{2,1,0:T(8,128)} %b_in.1, f32[128,128]{1,0:T(8,128)} %constant.16.clone.fwd_in, f32[128,128]{1,0:T(8,128)} %constant.17.clone.inv_in, f32[32,64,128]{2,1,0:T(8,128)} %constant.18.clone.turn_in, f32[32,16,128]{2,1,0:T(8,128)} %constant.19.clone.wind_in, ...), custom_call_target="tpu_custom_call" | custom-call | tf_op jit(solution)/shard_map/pallas_call | solution.py:649
  41.0 1.7 %copy.12 = f32[8,16,512]{2,1,0:T(8,128)} copy(f32[8,16,512]{2,1,0:T(8,128)} %shard_map.100) | data formatting | bytes 524288
